TPU v7x, 128 devices: a whole 4x4x4 slice. The times are simulated.
128 devices in a mesh: ctx: 16 (over y, x_lo, core), dp: 8 (over x_hi, z).
Axes of the slice: x: 4 (x_hi: 2, x_lo: 2; x = x_hi * 2 + x_lo), y: 4, z: 4, core: 2. Of those that a mesh axis runs over, the one named last changes fastest.
Arguments:
- projected: bfloat16 [3, 4096, 4096], P(None, 'dp', 'ctx'), may hold values from -6 to 6
- filters: float32 [256, 4096], P(None, ('ctx', 'dp')), may hold values from -0.125 to 0.125
- cotangent: bfloat16 [4096, 4096], P('dp', 'ctx'), may hold values from -6 to 6
Outputs:
- mixed: bfloat16 [4096, 4096], P('dp', 'ctx')
- proj_grad: bfloat16 [3, 4096, 4096], P(None, 'dp', 'ctx')
- filter_grad: float32 [256, 4096], P(None, ('ctx', 'dp'))
All inputs are finite; a program needn't handle non-finite values.
Results may differ from a plain program's by a relative error of at most 0.0017.
Values sent between devices are 32-bit elements; how exact they have to be, the bound alone decides.
A program may use at most 64 MiB of HBM per device.

v0:
```python
import math

import jax
import jax.numpy as jnp
from jax import lax
from jax.sharding import PartitionSpec as P

GROUP = 16


def from_partner(value, axis, bit):
    mask = 2**bit
    pairs = [(source, source ^ mask) for source in range(lax.axis_size(axis))]
    return lax.ppermute(value, axis, pairs)


def exact_dot(left, right):
    return jnp.dot(left, right, precision=lax.Precision.HIGHEST)


def complex_table(size, sign):
    offsets = jnp.arange(size, dtype=jnp.int32)
    product_idx = offsets[:, None] * offsets[None, :] % size
    phase_angle = sign * 2.0 * math.pi * product_idx.astype(jnp.float32) / size
    return (jnp.cos(phase_angle), jnp.sin(phase_angle))


def complex_dot(real_part, imag_part, table_cos, table_sin):
    lead_dims = real_part.shape[:-1]
    flat_re = real_part.reshape(-1, real_part.shape[-1])
    flat_im = imag_part.reshape(-1, imag_part.shape[-1])
    out_re = exact_dot(flat_re, table_cos) - exact_dot(flat_im, table_sin)
    out_im = exact_dot(flat_re, table_sin) + exact_dot(flat_im, table_cos)
    return (
        out_re.reshape(lead_dims + (table_cos.shape[1],)),
        out_im.reshape(lead_dims + (table_cos.shape[1],)),
    )


def rotate(real_part, imag_part, cos_turn, sin_turn):
    return (
        real_part * cos_turn - imag_part * sin_turn,
        real_part * sin_turn + imag_part * cos_turn,
    )


def reverse_bits(ctx_index, bit_count):
    result = jnp.zeros((), jnp.int32)
    for bit_level in range(bit_count):
        result = result + jnp.left_shift(
            jnp.bitwise_and(jnp.right_shift(ctx_index, bit_level), 1), bit_count - 1 - bit_level
        )
    return result


def forward_pairs(real_part, imag_part, ctx_index, ctx_count):
    bit_count = ctx_count.bit_length() - 1
    for bit_level in range(bit_count):
        half_span = ctx_count >> bit_level + 1
        other_re, other_im = from_partner((real_part, imag_part), "ctx", bit_count - 1 - bit_level)
        is_upper = jnp.bitwise_and(ctx_index, half_span) != 0
        within = jnp.bitwise_and(ctx_index, half_span - 1).astype(jnp.float32)
        phase_angle = -math.pi * within / half_span
        turned_re, turned_im = rotate(
            other_re - real_part, other_im - imag_part, jnp.cos(phase_angle), jnp.sin(phase_angle)
        )
        real_part = jnp.where(is_upper, turned_re, real_part + other_re)
        imag_part = jnp.where(is_upper, turned_im, imag_part + other_im)
    return (real_part, imag_part)


def inverse_pairs(real_part, imag_part, ctx_index, ctx_count):
    bit_count = ctx_count.bit_length() - 1
    for bit_level in range(bit_count):
        half_span = 1 << bit_level
        other_re, other_im = from_partner((real_part, imag_part), "ctx", bit_level)
        is_upper = jnp.bitwise_and(ctx_index, half_span) != 0
        within = jnp.bitwise_and(ctx_index, half_span - 1).astype(jnp.float32)
        phase_angle = math.pi * within / half_span
        first_re = jnp.where(is_upper, other_re, real_part)
        first_im = jnp.where(is_upper, other_im, imag_part)
        second_re = jnp.where(is_upper, real_part, other_re)
        second_im = jnp.where(is_upper, imag_part, other_im)
        turned_re, turned_im = rotate(
            second_re, second_im, jnp.cos(phase_angle), jnp.sin(phase_angle)
        )
        real_part = jnp.where(is_upper, first_re - turned_re, first_re + turned_re) * 0.5
        imag_part = jnp.where(is_upper, first_im - turned_im, first_im + turned_im) * 0.5
    return (real_part, imag_part)


def frequency_row(ctx_index, ctx_count):
    return reverse_bits(ctx_index, ctx_count.bit_length() - 1)


def to_spectrum(signal, ctx_index, ctx_count):
    block_len = signal.shape[-1]
    length = block_len * ctx_count
    offsets = jnp.arange(block_len, dtype=jnp.int32)
    position = (ctx_index * block_len + offsets).astype(jnp.float32)
    half_phase = -math.pi * position / length
    real_part = jnp.stack([signal, signal * jnp.cos(half_phase)])
    imag_part = jnp.stack([jnp.zeros_like(signal), signal * jnp.sin(half_phase)])
    real_part, imag_part = forward_pairs(real_part, imag_part, ctx_index, ctx_count)
    freq_row = frequency_row(ctx_index, ctx_count)
    twist = -2.0 * math.pi * (offsets * freq_row).astype(jnp.float32) / length
    real_part, imag_part = rotate(real_part, imag_part, jnp.cos(twist), jnp.sin(twist))
    table_cos, table_sin = complex_table(block_len, -1.0)
    return complex_dot(real_part, imag_part, table_cos, table_sin)


def from_spectrum(real_part, imag_part, ctx_index, ctx_count):
    block_len = real_part.shape[-1]
    length = block_len * ctx_count
    offsets = jnp.arange(block_len, dtype=jnp.int32)
    table_cos, table_sin = complex_table(block_len, 1.0)
    real_part, imag_part = complex_dot(real_part, imag_part, table_cos, table_sin)
    freq_row = frequency_row(ctx_index, ctx_count)
    twist = 2.0 * math.pi * (offsets * freq_row).astype(jnp.float32) / length
    real_part, imag_part = rotate(
        real_part / block_len, imag_part / block_len, jnp.cos(twist), jnp.sin(twist)
    )
    real_part, imag_part = inverse_pairs(real_part, imag_part, ctx_index, ctx_count)
    position = (ctx_index * block_len + offsets).astype(jnp.float32)
    half_phase = math.pi * position / length
    return 0.5 * (
        real_part[0] + real_part[1] * jnp.cos(half_phase) - imag_part[1] * jnp.sin(half_phase)
    )


def on_device(projected, filters, cotangent):
    ctx_count = lax.axis_size("ctx")
    ctx_index = lax.axis_index("ctx")
    block_len = cotangent.shape[1]
    channels = cotangent.shape[0]
    groups = channels // GROUP
    filter_rows = lax.all_to_all(filters, "dp", split_axis=0, concat_axis=1, tiled=True)
    features = projected.astype(jnp.float32)
    gate_query = features[0]
    key_part = features[1]
    value_part = features[2]
    product = key_part * value_part
    prod_re, prod_im = to_spectrum(product, ctx_index, ctx_count)
    filt_re, filt_im = to_spectrum(filter_rows, ctx_index, ctx_count)
    prod_re = prod_re.reshape(2, groups, GROUP, block_len)
    prod_im = prod_im.reshape(2, groups, GROUP, block_len)
    filt_re = filt_re[:, :, None, :]
    filt_im = filt_im[:, :, None, :]
    conv_re = (prod_re * filt_re - prod_im * filt_im).reshape(2, channels, block_len)
    conv_im = (prod_re * filt_im + prod_im * filt_re).reshape(2, channels, block_len)
    conv = from_spectrum(conv_re, conv_im, ctx_index, ctx_count)
    mixed = (gate_query * conv).astype(jnp.bfloat16)
    cot_values = cotangent.astype(jnp.float32)
    gate_grad = cot_values * conv
    conv_cot = cot_values * gate_query
    cot_re, cot_im = to_spectrum(conv_cot, ctx_index, ctx_count)
    cot_re = cot_re.reshape(2, groups, GROUP, block_len)
    cot_im = cot_im.reshape(2, groups, GROUP, block_len)
    back_re = (filt_re * cot_re + filt_im * cot_im).reshape(2, channels, block_len)
    back_im = (filt_re * cot_im - filt_im * cot_re).reshape(2, channels, block_len)
    product_grad = from_spectrum(back_re, back_im, ctx_index, ctx_count)
    lag_re = jnp.sum(prod_re * cot_re + prod_im * cot_im, axis=2)
    lag_im = jnp.sum(prod_re * cot_im - prod_im * cot_re, axis=2)
    filter_time = from_spectrum(lag_re, lag_im, ctx_index, ctx_count)
    filter_grad = lax.all_to_all(filter_time, "dp", split_axis=1, concat_axis=0, tiled=True)
    proj_grad = jnp.stack([gate_grad, product_grad * value_part, product_grad * key_part]).astype(
        jnp.bfloat16
    )
    return (mixed, proj_grad, filter_grad)


def solution(mesh):
    in_specs = (P(None, "dp", "ctx"), P(None, ("ctx", "dp")), P("dp", "ctx"))
    out_specs = (P("dp", "ctx"), P(None, "dp", "ctx"), P(None, ("ctx", "dp")))
    return jax.shard_map(
        on_device, mesh=mesh, in_specs=in_specs, out_specs=out_specs, check_vma=False
    )
```

profile of v0, /device:TPU:1, one launch (start us, length us, event | category | flops | bytes accessed | tf_op | source)
XLA Modules:
  0.0 662.7 jit_solution(16498158495075827306)
XLA Ops:
  3.1 3.7 collective-permute-start.24
  8.1 21.7 %collective-permute-done.24 = f32[2,512,256]{2,1,0:T(8,128)} collective-permute-done((f32[2,512,256]{2,1,0:T(8,128)}, f32[2,512,256]{2,1,0:T(8,128)}, u32[]{:S(2)}, u32[]{:S(2)}) %collective-permute-start.24) | collective-permute-done | bytes 1048608 | tf_op jit(solution)/shard_map/ppermute | solution.py:14
  29.8 22.5 %collective-permute-done.25 = f32[2,512,256]{2,1,0:T(8,128)} collective-permute-done((f32[2,512,256]{2,1,0:T(8,128)}, f32[2,512,256]{2,1,0:T(8,128)}, u32[]{:S(2)}, u32[]{:S(2)}) %collective-permute-start.25) | collective-permute-done | bytes 1048608 | tf_op jit(solution)/shard_map/ppermute | solution.py:14
  52.3 3.2 add_select_fusion.6
  57.9 7.5 %all-to-all-start = ((f32[8,1,1024]{2,1,0:T(1,128)}), f32[8,1,1024]{2,1,0:T(1,128)S(1)}, u32[]{:S(2)}, u32[]{:S(2)}) async-start(f32[8,1,1024]{2,1,0:T(1,128)} %reshape.232), calls=%async_computation | async-start | bytes 65536 | tf_op jit(solution)/shard_map/all_to_all | solution.py:137
  65.5 6.5 all-to-all-done
  73.5 3.0 collective-permute-start.8
  79.9 21.6 %collective-permute-done.27 = f32[2,512,256]{2,1,0:T(8,128)} collective-permute-done((f32[2,512,256]{2,1,0:T(8,128)}, f32[2,512,256]{2,1,0:T(8,128)}, u32[]{:S(2)}, u32[]{:S(2)}) %collective-permute-start.27) | collective-permute-done | bytes 1048608 | tf_op jit(solution)/shard_map/ppermute | solution.py:14
  101.5 3.6 add_select_fusion.4
  112.6 37.4 %collective-permute-done.12 = f32[2,32,256]{2,1,0:T(8,128)S(1)} collective-permute-done((f32[2,32,256]{2,1,0:T(8,128)S(1)}, f32[2,32,256]{2,1,0:T(8,128)S(1)}, u32[]{:S(2)}, u32[]{:S(2)}) %collective-permute-start.12) | collective-permute-done | bytes 65568 | tf_op jit(solution)/shard_map/ppermute | solution.py:14
  151.5 4.7 collective-permute-start.14
  172.4 3.3 fusion.3
  191.8 23.1 %collective-permute-done.34 = f32[2,512,256]{2,1,0:T(8,128)} collective-permute-done((f32[2,512,256]{2,1,0:T(8,128)}, f32[2,512,256]{2,1,0:T(8,128)}, u32[]{:S(2)}, u32[]{:S(2)}) %collective-permute-start.34) | collective-permute-done | bytes 1048608 | tf_op jit(solution)/shard_map/ppermute | solution.py:14
  214.9 22.5 %collective-permute-done.35 = f32[2,512,256]{2,1,0:T(8,128)} collective-permute-done((f32[2,512,256]{2,1,0:T(8,128)}, f32[2,512,256]{2,1,0:T(8,128)}, u32[]{:S(2)}, u32[]{:S(2)}) %collective-permute-start.35) | collective-permute-done | bytes 1048608 | tf_op jit(solution)/shard_map/ppermute | solution.py:14
  237.4 4.1 select_multiply_fusion.3
  243.1 22.4 %collective-permute-done.36 = f32[2,512,256]{2,1,0:T(8,128)} collective-permute-done((f32[2,512,256]{2,1,0:T(8,128)}, f32[2,512,256]{2,1,0:T(8,128)}, u32[]{:S(2)}, u32[]{:S(2)}) %collective-permute-start.36) | collective-permute-done | bytes 1048608 | tf_op jit(solution)/shard_map/ppermute | solution.py:14
  265.5 22.5 %collective-permute-done.37 = f32[2,512,256]{2,1,0:T(8,128)} collective-permute-done((f32[2,512,256]{2,1,0:T(8,128)}, f32[2,512,256]{2,1,0:T(8,128)}, u32[]{:S(2)}, u32[]{:S(2)}) %collective-permute-start.37) | collective-permute-done | bytes 1048608 | tf_op jit(solution)/shard_map/ppermute | solution.py:14
  288.0 4.1 select_multiply_fusion.1
  295.3 21.4 %collective-permute-done.38 = f32[2,512,256]{2,1,0:T(8,128)} collective-permute-done((f32[2,512,256]{2,1,0:T(8,128)}, f32[2,512,256]{2,1,0:T(8,128)}, u32[]{:S(2)}, u32[]{:S(2)}) %collective-permute-start.38) | collective-permute-done | bytes 1048608 | tf_op jit(solution)/shard_map/ppermute | solution.py:14
  316.7 22.5 %collective-permute-done.39 = f32[2,512,256]{2,1,0:T(8,128)} collective-permute-done((f32[2,512,256]{2,1,0:T(8,128)}, f32[2,512,256]{2,1,0:T(8,128)}, u32[]{:S(2)}, u32[]{:S(2)}) %collective-permute-start.39) | collective-permute-done | bytes 1048608 | tf_op jit(solution)/shard_map/ppermute | solution.py:14
  346.4 20.2 %collective-permute-done = f32[2,512,256]{2,1,0:T(8,128)S(1)} collective-permute-done((f32[2,512,256]{2,1,0:T(8,128)S(1)}, f32[2,512,256]{2,1,0:T(8,128)S(1)}, u32[]{:S(2)}, u32[]{:S(2)}) %collective-permute-start) | collective-permute-done | bytes 1048608 | tf_op jit(solution)/shard_map/ppermute | solution.py:14
  366.6 22.5 %collective-permute-done.1 = f32[2,512,256]{2,1,0:T(8,128)S(1)} collective-permute-done((f32[2,512,256]{2,1,0:T(8,128)S(1)}, f32[2,512,256]{2,1,0:T(8,128)S(1)}, u32[]{:S(2)}, u32[]{:S(2)}) %collective-permute-start.1) | collective-permute-done | bytes 1048608 | tf_op jit(solution)/shard_map/ppermute | solution.py:14
  391.1 20.4 %collective-permute-done.2 = f32[2,512,256]{2,1,0:T(8,128)S(1)} collective-permute-done((f32[2,512,256]{2,1,0:T(8,128)S(1)}, f32[2,512,256]{2,1,0:T(8,128)S(1)}, u32[]{:S(2)}, u32[]{:S(2)}) %collective-permute-start.2) | collective-permute-done | bytes 1048608 | tf_op jit(solution)/shard_map/ppermute | solution.py:14
  411.4 22.5 %collective-permute-done.3 = f32[2,512,256]{2,1,0:T(8,128)S(1)} collective-permute-done((f32[2,512,256]{2,1,0:T(8,128)S(1)}, f32[2,512,256]{2,1,0:T(8,128)S(1)}, u32[]{:S(2)}, u32[]{:S(2)}) %collective-permute-start.3) | collective-permute-done | bytes 1048608 | tf_op jit(solution)/shard_map/ppermute | solution.py:14
  435.9 19.0 %collective-permute-done.4 = f32[2,512,256]{2,1,0:T(8,128)S(1)} collective-permute-done((f32[2,512,256]{2,1,0:T(8,128)S(1)}, f32[2,512,256]{2,1,0:T(8,128)S(1)}, u32[]{:S(2)}, u32[]{:S(2)}) %collective-permute-start.4) | collective-permute-done | bytes 1048608 | tf_op jit(solution)/shard_map/ppermute | solution.py:14
  454.9 22.5 %collective-permute-done.5 = f32[2,512,256]{2,1,0:T(8,128)S(1)} collective-permute-done((f32[2,512,256]{2,1,0:T(8,128)S(1)}, f32[2,512,256]{2,1,0:T(8,128)S(1)}, u32[]{:S(2)}, u32[]{:S(2)}) %collective-permute-start.5) | collective-permute-done | bytes 1048608 | tf_op jit(solution)/shard_map/ppermute | solution.py:14
  477.8 5.2 collective-permute-start.6
  516.3 16.9 %collective-permute-done.18 = f32[2,512,256]{2,1,0:T(8,128)S(1)} collective-permute-done((f32[2,512,256]{2,1,0:T(8,128)S(1)}, f32[2,512,256]{2,1,0:T(8,128)S(1)}, u32[]{:S(2)}, u32[]{:S(2)}) %collective-permute-start.18) | collective-permute-done | bytes 1048608 | tf_op jit(solution)/shard_map/ppermute | solution.py:14
  533.1 22.5 %collective-permute-done.19 = f32[2,512,256]{2,1,0:T(8,128)S(1)} collective-permute-done((f32[2,512,256]{2,1,0:T(8,128)S(1)}, f32[2,512,256]{2,1,0:T(8,128)S(1)}, u32[]{:S(2)}, u32[]{:S(2)}) %collective-permute-start.19) | collective-permute-done | bytes 1048608 | tf_op jit(solution)/shard_map/ppermute | solution.py:14
  567.5 36.1 %collective-permute-done.44 = f32[2,32,256]{2,1,0:T(8,128)S(1)} collective-permute-done((f32[2,32,256]{2,1,0:T(8,128)S(1)}, f32[2,32,256]{2,1,0:T(8,128)S(1)}, u32[]{:S(2)}, u32[]{:S(2)}) %collective-permute-start.44) | collective-permute-done | bytes 65568 | tf_op jit(solution)/shard_map/ppermute | solution.py:14
  622.2 13.9 %all_to_all.32 = f32[8,1,1024]{2,1,0:T(1,128)S(1)} all-to-all(f32[8,1,1024]{2,1,0:T(1,128)S(1)} %reshape.234), channel_id=1, replica_groups=mesh['ctx'=16,'dp'=8] {'dp'}, dimensions={0} | all-to-all | bytes 65536 | tf_op jit(solution)/shard_map/all_to_all | solution.py:165
  639.2 18.1 %collective-permute-done.23 = f32[2,512,256]{2,1,0:T(8,128)} collective-permute-done((f32[2,512,256]{2,1,0:T(8,128)S(1)}, f32[2,512,256]{2,1,0:T(8,128)}, u32[]{:S(2)}, u32[]{:S(2)}) %collective-permute-start.23) | collective-permute-done | bytes 1048608 | tf_op jit(solution)/shard_map/ppermute | solution.py:14
  (189 shorter events, 139.5 us)
Async XLA Ops:
  3.1 26.7 %collective-permute-start.24 = (f32[2,512,256]{2,1,0:T(8,128)}, f32[2,512,256]{2,1,0:T(8,128)}, u32[]{:S(2)}, u32[]{:S(2)}) collective-permute-start(f32[2,512,256]{2,1,0:T(8,128)} %pad_maximum_fusion.1), channel_id=1, source_target_pairs={{0,64},{8,72},{16,80},{24,88},{32,96},{40,104},{48,112},{56,120},{... | collective-permute-start | bytes 3145736 | tf_op jit(solution)/shard_map/ppermute | solution.py:14
  7.9 44.3 %collective-permute-start.25 = (f32[2,512,256]{2,1,0:T(8,128)}, f32[2,512,256]{2,1,0:T(8,128)}, u32[]{:S(2)}, u32[]{:S(2)}) collective-permute-start(f32[2,512,256]{2,1,0:T(8,128)} %stack.55), channel_id=1, source_target_pairs={{0,64},{8,72},{16,80},{24,88},{32,96},{40,104},{48,112},{56,120},{... | collective-permute-start | bytes 3145736 | tf_op jit(solution)/shard_map/ppermute | solution.py:14
  55.5 23.3 %collective-permute-start.26 = (f32[2,512,256]{2,1,0:T(8,128)}, f32[2,512,256]{2,1,0:T(8,128)S(1)}, u32[]{:S(2)}, u32[]{:S(2)}) collective-permute-start(f32[2,512,256]{2,1,0:T(8,128)} %get-tuple-element.47), channel_id=1, source_target_pairs={{0,32},{8,40},{16,48},{24,56},{32,0},{40,8},{48,16},{56,24},{64,96... | collective-permute-start | bytes 3145736 | tf_op jit(solution)/shard_map/ppermute | solution.py:14
  56.8 44.6 %collective-permute-start.27 = (f32[2,512,256]{2,1,0:T(8,128)}, f32[2,512,256]{2,1,0:T(8,128)}, u32[]{:S(2)}, u32[]{:S(2)}) collective-permute-start(f32[2,512,256]{2,1,0:T(8,128)} %get-tuple-element.46), channel_id=1, source_target_pairs={{0,32},{8,40},{16,48},{24,56},{32,0},{40,8},{48,16},{56,24},{64,96... | collective-permute-start | bytes 3145736 | tf_op jit(solution)/shard_map/ppermute | solution.py:14
  57.9 14.1 %all-to-all-start = ((f32[8,1,1024]{2,1,0:T(1,128)}), f32[8,1,1024]{2,1,0:T(1,128)S(1)}, u32[]{:S(2)}, u32[]{:S(2)}) async-start(f32[8,1,1024]{2,1,0:T(1,128)} %reshape.232), calls=%async_computation | async-start | bytes 65536 | tf_op jit(solution)/shard_map/all_to_all | solution.py:137
  73.5 32.9 %collective-permute-start.8 = (f32[2,32,256]{2,1,0:T(8,128)S(1)}, f32[2,32,256]{2,1,0:T(8,128)S(1)}, u32[]{:S(2)}, u32[]{:S(2)}) collective-permute-start(f32[2,32,256]{2,1,0:T(8,128)S(1)} %pad_maximum_fusion.3), channel_id=1, source_target_pairs={{0,64},{8,72},{16,80},{24,88},{32,96},{40,104},{48,112},{56,120},{... | collective-permute-start | bytes 196616 | tf_op jit(solution)/shard_map/ppermute | solution.py:14
  76.5 29.9 %collective-permute-start.9 = (f32[2,32,256]{2,1,0:T(8,128)S(1)}, f32[2,32,256]{2,1,0:T(8,128)S(1)}, u32[]{:S(2)}, u32[]{:S(2)}) collective-permute-start(f32[2,32,256]{2,1,0:T(8,128)S(1)} %stack.49), channel_id=1, source_target_pairs={{0,64},{8,72},{16,80},{24,88},{32,96},{40,104},{48,112},{56,120},{... | collective-permute-start | bytes 196616 | tf_op jit(solution)/shard_map/ppermute | solution.py:14
  105.0 52.5 %collective-permute-start.28 = (f32[2,512,256]{2,1,0:T(8,128)}, f32[2,512,256]{2,1,0:T(8,128)}, u32[]{:S(2)}, u32[]{:S(2)}) collective-permute-start(f32[2,512,256]{2,1,0:T(8,128)} %get-tuple-element.35), channel_id=1, source_target_pairs={{0,16},{8,24},{16,0},{24,8},{32,48},{40,56},{48,32},{56,40},{64,80... | collective-permute-start | bytes 3145736 | tf_op jit(solution)/shard_map/ppermute | solution.py:14
  106.2 51.3 %collective-permute-start.29 = (f32[2,512,256]{2,1,0:T(8,128)S(1)}, f32[2,512,256]{2,1,0:T(8,128)}, u32[]{:S(2)}, u32[]{:S(2)}) collective-permute-start(f32[2,512,256]{2,1,0:T(8,128)S(1)} %get-tuple-element.34), channel_id=1, source_target_pairs={{0,16},{8,24},{16,0},{24,8},{32,48},{40,56},{48,32},{56,40},{64,80... | collective-permute-start | bytes 3145736 | tf_op jit(solution)/shard_map/ppermute | solution.py:14
  111.0 39.0 %collective-permute-start.12 = (f32[2,32,256]{2,1,0:T(8,128)S(1)}, f32[2,32,256]{2,1,0:T(8,128)S(1)}, u32[]{:S(2)}, u32[]{:S(2)}) collective-permute-start(f32[2,32,256]{2,1,0:T(8,128)S(1)} %get-tuple-element.73), channel_id=1, source_target_pairs={{0,16},{8,24},{16,0},{24,8},{32,48},{40,56},{48,32},{56,40},{64,80... | collective-permute-start | bytes 196616 | tf_op jit(solution)/shard_map/ppermute | solution.py:14
  112.3 39.1 %collective-permute-start.13 = (f32[2,32,256]{2,1,0:T(8,128)S(1)}, f32[2,32,256]{2,1,0:T(8,128)S(1)}, u32[]{:S(2)}, u32[]{:S(2)}) collective-permute-start(f32[2,32,256]{2,1,0:T(8,128)S(1)} %get-tuple-element.72), channel_id=1, source_target_pairs={{0,16},{8,24},{16,0},{24,8},{32,48},{40,56},{48,32},{56,40},{64,80... | collective-permute-start | bytes 196616 | tf_op jit(solution)/shard_map/ppermute | solution.py:14
  190.0 24.9 %collective-permute-start.34 = (f32[2,512,256]{2,1,0:T(8,128)}, f32[2,512,256]{2,1,0:T(8,128)}, u32[]{:S(2)}, u32[]{:S(2)}) collective-permute-start(f32[2,512,256]{2,1,0:T(8,128)} %get-tuple-element.31), channel_id=1, source_target_pairs={{0,16},{8,24},{16,0},{24,8},{32,48},{40,56},{48,32},{56,40},{64,80... | collective-permute-start | bytes 3145736 | tf_op jit(solution)/shard_map/ppermute | solution.py:14
  191.2 46.2 %collective-permute-start.35 = (f32[2,512,256]{2,1,0:T(8,128)}, f32[2,512,256]{2,1,0:T(8,128)}, u32[]{:S(2)}, u32[]{:S(2)}) collective-permute-start(f32[2,512,256]{2,1,0:T(8,128)} %get-tuple-element.30), channel_id=1, source_target_pairs={{0,16},{8,24},{16,0},{24,8},{32,48},{40,56},{48,32},{56,40},{64,80... | collective-permute-start | bytes 3145736 | tf_op jit(solution)/shard_map/ppermute | solution.py:14
  241.5 24.0 %collective-permute-start.36 = (f32[2,512,256]{2,1,0:T(8,128)}, f32[2,512,256]{2,1,0:T(8,128)}, u32[]{:S(2)}, u32[]{:S(2)}) collective-permute-start(f32[2,512,256]{2,1,0:T(8,128)} %get-tuple-element.29), channel_id=1, source_target_pairs={{0,32},{8,40},{16,48},{24,56},{32,0},{40,8},{48,16},{56,24},{64,96... | collective-permute-start | bytes 3145736 | tf_op jit(solution)/shard_map/ppermute | solution.py:14
  242.8 45.2 %collective-permute-start.37 = (f32[2,512,256]{2,1,0:T(8,128)}, f32[2,512,256]{2,1,0:T(8,128)}, u32[]{:S(2)}, u32[]{:S(2)}) collective-permute-start(f32[2,512,256]{2,1,0:T(8,128)} %get-tuple-element.28), channel_id=1, source_target_pairs={{0,32},{8,40},{16,48},{24,56},{32,0},{40,8},{48,16},{56,24},{64,96... | collective-permute-start | bytes 3145736 | tf_op jit(solution)/shard_map/ppermute | solution.py:14
  292.1 24.6 %collective-permute-start.38 = (f32[2,512,256]{2,1,0:T(8,128)}, f32[2,512,256]{2,1,0:T(8,128)}, u32[]{:S(2)}, u32[]{:S(2)}) collective-permute-start(f32[2,512,256]{2,1,0:T(8,128)} %get-tuple-element.27), channel_id=1, source_target_pairs={{0,64},{8,72},{16,80},{24,88},{32,96},{40,104},{48,112},{56,120},{... | collective-permute-start | bytes 3145736 | tf_op jit(solution)/shard_map/ppermute | solution.py:14
  295.0 44.2 %collective-permute-start.39 = (f32[2,512,256]{2,1,0:T(8,128)}, f32[2,512,256]{2,1,0:T(8,128)}, u32[]{:S(2)}, u32[]{:S(2)}) collective-permute-start(f32[2,512,256]{2,1,0:T(8,128)} %get-tuple-element.26), channel_id=1, source_target_pairs={{0,64},{8,72},{16,80},{24,88},{32,96},{40,104},{48,112},{56,120},{... | collective-permute-start | bytes 3145736 | tf_op jit(solution)/shard_map/ppermute | solution.py:14
  343.2 23.4 %collective-permute-start = (f32[2,512,256]{2,1,0:T(8,128)S(1)}, f32[2,512,256]{2,1,0:T(8,128)S(1)}, u32[]{:S(2)}, u32[]{:S(2)}) collective-permute-start(f32[2,512,256]{2,1,0:T(8,128)S(1)} %pad_maximum_fusion), channel_id=1, source_target_pairs={{0,64},{8,72},{16,80},{24,88},{32,96},{40,104},{48,112},{56,120},{... | collective-permute-start | bytes 3145736 | tf_op jit(solution)/shard_map/ppermute | solution.py:14
  346.2 42.9 %collective-permute-start.1 = (f32[2,512,256]{2,1,0:T(8,128)S(1)}, f32[2,512,256]{2,1,0:T(8,128)S(1)}, u32[]{:S(2)}, u32[]{:S(2)}) collective-permute-start(f32[2,512,256]{2,1,0:T(8,128)S(1)} %stack.46), channel_id=1, source_target_pairs={{0,64},{8,72},{16,80},{24,88},{32,96},{40,104},{48,112},{56,120},{... | collective-permute-start | bytes 3145736 | tf_op jit(solution)/shard_map/ppermute | solution.py:14
  389.5 21.9 %collective-permute-start.2 = (f32[2,512,256]{2,1,0:T(8,128)S(1)}, f32[2,512,256]{2,1,0:T(8,128)S(1)}, u32[]{:S(2)}, u32[]{:S(2)}) collective-permute-start(f32[2,512,256]{2,1,0:T(8,128)S(1)} %get-tuple-element.49), channel_id=1, source_target_pairs={{0,32},{8,40},{16,48},{24,56},{32,0},{40,8},{48,16},{56,24},{64,96... | collective-permute-start | bytes 3145736 | tf_op jit(solution)/shard_map/ppermute | solution.py:14
  390.9 43.0 %collective-permute-start.3 = (f32[2,512,256]{2,1,0:T(8,128)S(1)}, f32[2,512,256]{2,1,0:T(8,128)S(1)}, u32[]{:S(2)}, u32[]{:S(2)}) collective-permute-start(f32[2,512,256]{2,1,0:T(8,128)S(1)} %get-tuple-element.48), channel_id=1, source_target_pairs={{0,32},{8,40},{16,48},{24,56},{32,0},{40,8},{48,16},{56,24},{64,96... | collective-permute-start | bytes 3145736 | tf_op jit(solution)/shard_map/ppermute | solution.py:14
  434.3 20.5 %collective-permute-start.4 = (f32[2,512,256]{2,1,0:T(8,128)S(1)}, f32[2,512,256]{2,1,0:T(8,128)S(1)}, u32[]{:S(2)}, u32[]{:S(2)}) collective-permute-start(f32[2,512,256]{2,1,0:T(8,128)S(1)} %get-tuple-element.45), channel_id=1, source_target_pairs={{0,16},{8,24},{16,0},{24,8},{32,48},{40,56},{48,32},{56,40},{64,80... | collective-permute-start | bytes 3145736 | tf_op jit(solution)/shard_map/ppermute | solution.py:14
  435.6 41.8 %collective-permute-start.5 = (f32[2,512,256]{2,1,0:T(8,128)S(1)}, f32[2,512,256]{2,1,0:T(8,128)S(1)}, u32[]{:S(2)}, u32[]{:S(2)}) collective-permute-start(f32[2,512,256]{2,1,0:T(8,128)S(1)} %get-tuple-element.44), channel_id=1, source_target_pairs={{0,16},{8,24},{16,0},{24,8},{32,48},{40,56},{48,32},{56,40},{64,80... | collective-permute-start | bytes 3145736 | tf_op jit(solution)/shard_map/ppermute | solution.py:14
  508.7 24.5 %collective-permute-start.18 = (f32[2,512,256]{2,1,0:T(8,128)S(1)}, f32[2,512,256]{2,1,0:T(8,128)S(1)}, u32[]{:S(2)}, u32[]{:S(2)}) collective-permute-start(f32[2,512,256]{2,1,0:T(8,128)S(1)} %get-tuple-element.41), channel_id=1, source_target_pairs={{0,16},{8,24},{16,0},{24,8},{32,48},{40,56},{48,32},{56,40},{64,80... | collective-permute-start | bytes 3145736 | tf_op jit(solution)/shard_map/ppermute | solution.py:14
  510.0 45.7 %collective-permute-start.19 = (f32[2,512,256]{2,1,0:T(8,128)S(1)}, f32[2,512,256]{2,1,0:T(8,128)S(1)}, u32[]{:S(2)}, u32[]{:S(2)}) collective-permute-start(f32[2,512,256]{2,1,0:T(8,128)S(1)} %get-tuple-element.40), channel_id=1, source_target_pairs={{0,16},{8,24},{16,0},{24,8},{32,48},{40,56},{48,32},{56,40},{64,80... | collective-permute-start | bytes 3145736 | tf_op jit(solution)/shard_map/ppermute | solution.py:14
  556.2 51.9 %collective-permute-start.20 = (f32[2,512,256]{2,1,0:T(8,128)S(1)}, f32[2,512,256]{2,1,0:T(8,128)S(1)}, u32[]{:S(2)}, u32[]{:S(2)}) collective-permute-start(f32[2,512,256]{2,1,0:T(8,128)S(1)} %get-tuple-element.39), channel_id=1, source_target_pairs={{0,32},{8,40},{16,48},{24,56},{32,0},{40,8},{48,16},{56,24},{64,96... | collective-permute-start | bytes 3145736 | tf_op jit(solution)/shard_map/ppermute | solution.py:14
  557.2 51.0 %collective-permute-start.21 = (f32[2,512,256]{2,1,0:T(8,128)S(1)}, f32[2,512,256]{2,1,0:T(8,128)S(1)}, u32[]{:S(2)}, u32[]{:S(2)}) collective-permute-start(f32[2,512,256]{2,1,0:T(8,128)S(1)} %get-tuple-element.38), channel_id=1, source_target_pairs={{0,32},{8,40},{16,48},{24,56},{32,0},{40,8},{48,16},{56,24},{64,96... | collective-permute-start | bytes 3145736 | tf_op jit(solution)/shard_map/ppermute | solution.py:14
  565.9 37.7 %collective-permute-start.44 = (f32[2,32,256]{2,1,0:T(8,128)S(1)}, f32[2,32,256]{2,1,0:T(8,128)S(1)}, u32[]{:S(2)}, u32[]{:S(2)}) collective-permute-start(f32[2,32,256]{2,1,0:T(8,128)S(1)} %get-tuple-element.67), channel_id=1, source_target_pairs={{0,32},{8,40},{16,48},{24,56},{32,0},{40,8},{48,16},{56,24},{64,96... | collective-permute-start | bytes 196616 | tf_op jit(solution)/shard_map/ppermute | solution.py:14
  566.9 38.2 %collective-permute-start.45 = (f32[2,32,256]{2,1,0:T(8,128)S(1)}, f32[2,32,256]{2,1,0:T(8,128)S(1)}, u32[]{:S(2)}, u32[]{:S(2)}) collective-permute-start(f32[2,32,256]{2,1,0:T(8,128)S(1)} %get-tuple-element.66), channel_id=1, source_target_pairs={{0,32},{8,40},{16,48},{24,56},{32,0},{40,8},{48,16},{56,24},{64,96... | collective-permute-start | bytes 196616 | tf_op jit(solution)/shard_map/ppermute | solution.py:14
  605.1 7.6 %collective-permute-start.46 = (f32[2,32,256]{2,1,0:T(8,128)S(1)}, f32[2,32,256]{2,1,0:T(8,128)S(1)}, u32[]{:S(2)}, u32[]{:S(2)}) collective-permute-start(f32[2,32,256]{2,1,0:T(8,128)S(1)} %get-tuple-element.65), channel_id=1, source_target_pairs={{0,64},{8,72},{16,80},{24,88},{32,96},{40,104},{48,112},{56,120},{... | collective-permute-start | bytes 196616 | tf_op jit(solution)/shard_map/ppermute | solution.py:14
  609.8 29.4 %collective-permute-start.22 = (f32[2,512,256]{2,1,0:T(8,128)}, f32[2,512,256]{2,1,0:T(8,128)}, u32[]{:S(2)}, u32[]{:S(2)}) collective-permute-start(f32[2,512,256]{2,1,0:T(8,128)} %get-tuple-element.37), channel_id=1, source_target_pairs={{0,64},{8,72},{16,80},{24,88},{32,96},{40,104},{48,112},{56,120},{... | collective-permute-start | bytes 3145736 | tf_op jit(solution)/shard_map/ppermute | solution.py:14
  611.6 45.6 %collective-permute-start.23 = (f32[2,512,256]{2,1,0:T(8,128)S(1)}, f32[2,512,256]{2,1,0:T(8,128)}, u32[]{:S(2)}, u32[]{:S(2)}) collective-permute-start(f32[2,512,256]{2,1,0:T(8,128)S(1)} %get-tuple-element.36), channel_id=1, source_target_pairs={{0,64},{8,72},{16,80},{24,88},{32,96},{40,104},{48,112},{56,120},{... | collective-permute-start | bytes 3145736 | tf_op jit(solution)/shard_map/ppermute | solution.py:14
  (31 other events, 324.2 us)
where the time goes:
time: 671 us; the launch traced here: 663 us
  waiting for transfers between devices  488 us (73%)
  starting transfers between devices  59.7 us (9%)
  other arithmetic  44 us (7%)
  matrix products  43.3 us (6%)
  blocking collectives  13.9 us (2%)
  local copies, waits for them, and re-layouts  10.9 us (2%)
    ppermute x48, waiting for transfers between devices, from_partner(): return lax.ppermute(value, axis, pairs)  482 us
    ppermute x48, starting transfers between devices, from_partner(): return lax.ppermute(value, axis, pairs)  52.2 us
    dot_general x24, matrix products, exact_dot(): return jnp.dot(left, right, precision=lax.Precision.HIGHEST)  43.3 us
    mul x10, other arithmetic, inverse_pairs(): jnp.where(is_upper, first_im - turned_im, first_im + turned_im) * 0.5  14.5 us
    all_to_all x1, blocking collectives, on_device(): lax.all_to_all(filter_time, 'dp', split_axis=1, concat_axis=0, tiled=True)  13.9 us
  transfers between devices with their start and end apart: 49, of which 38 were waited for; matrix products, arithmetic and copies ran while one was open for 5% of the time, Pallas kernels for 0%

commit v1 on v0

v1 whole, which is shorter than its diff:
```python
import functools

import jax
import jax.numpy as jnp
from jax import lax
from jax.experimental import pallas as pl
from jax.experimental.pallas import tpu as pltpu
from jax.sharding import PartitionSpec as P

MESH = pl.DeviceIdType.MESH
GROUP = 16
NC = 16
ND = 8
OWN = 2
BLK = 256
HALF = 128
F32 = jnp.float32
BF16 = jnp.bfloat16
NT = (((1,), (1,)), ((), ()))


def dot(left, right):
    return jnp.dot(left, right, preferred_element_type=F32)


def dot_nt(left, right):
    return lax.dot_general(left, right, NT, preferred_element_type=F32)


def split(value):
    high = value.astype(BF16)
    return high, (value - high.astype(F32)).astype(BF16)


def kernel(
    proj, filt, cot, mixed, pgrad, fgrad,
    sp, sq, rp, rq, yb, zb, cv, pv,
    fs, fd, ft, fr, hx, r1h, r1l,
    xh, xl, pth, ptl, qh, ql, s1, s2, fo, fa, fb, fc,
    ssem, rsem, dssem, drsem,
):
    me = lax.axis_index("ctx")
    dp = lax.axis_index("dp")

    def ctx_peer(o):
        return lax.rem(me + o, NC)

    def dp_peer(o):
        return lax.rem(dp + o, ND)

    def ctx_copy(kind, o, src, dst):
        return pltpu.make_async_remote_copy(
            src_ref=src, dst_ref=dst, send_sem=ssem.at[kind, o], recv_sem=rsem.at[kind, o],
            device_id=(ctx_peer(o), dp), device_id_type=MESH)

    def dp_copy(kind, o, src, dst):
        return pltpu.make_async_remote_copy(
            src_ref=src, dst_ref=dst, send_sem=dssem.at[kind, o], recv_sem=drsem.at[kind, o],
            device_id=(me, dp_peer(o)), device_id_type=MESH)

    def p_copy(o):
        return ctx_copy(0, o, sp.at[ctx_peer(o)], rp.at[:, me])

    def q_copy(o):
        return ctx_copy(1, o, sq.at[ctx_peer(o)], rq.at[:, me])

    def y_copy(g, o):
        return ctx_copy(2 + g, o, yb.at[g, ctx_peer(o)], cv.at[me, g])

    def z_copy(g, o):
        return ctx_copy(4 + g, o, zb.at[g, ctx_peer(o)], pv.at[me, g])

    def f_copy(o):
        return ctx_copy(6, o, ft.at[lax.div(ctx_peer(o), 2)], fr.at[me])

    def g_copy(o):
        return ctx_copy(7, o, fo.at[ctx_peer(o)], fa.at[me])

    def fd_copy(o):
        return dp_copy(0, o, fs.at[dp_peer(o)], fd.at[dp])

    def gd_copy(o):
        return dp_copy(1, o, fb.at[dp_peer(o)], fc.at[dp])

    def over(n, body):
        @pl.loop(1, n)
        def _(o):
            body(o)

    barrier = pltpu.get_barrier_semaphore()
    over(NC, lambda o: pl.semaphore_signal(
        barrier, inc=1, device_id=(ctx_peer(o), dp), device_id_type=MESH))
    over(ND, lambda o: pl.semaphore_signal(
        barrier, inc=1, device_id=(me, dp_peer(o)), device_id_type=MESH))

    fs[...] = jnp.concatenate(
        [filt[pl.ds(q, 64, stride=4), :] for q in range(4)], axis=1
    ).reshape(ND, 8, HALF)

    @pl.loop(0, NC)
    def _(k):
        rows = pl.ds(pl.multiple_of(k * 32, 32), 32)
        gate = proj[0, rows, :].astype(F32)
        prod = proj[1, rows, :].astype(F32) * proj[2, rows, :].astype(F32)
        ccot = cot[rows, :].astype(F32) * gate
        for g in range(OWN):
            for h in range(2):
                sp[k, g, h] = prod[g * 16 : g * 16 + 16, h * HALF : (h + 1) * HALF]
                sq[k, g, h] = ccot[g * 16 : g * 16 + 16, h * HALF : (h + 1) * HALF]

    pl.semaphore_wait(barrier, NC + ND - 2)
    over(ND, lambda o: fd_copy(o).start())
    over(NC, lambda o: p_copy(o).start())
    fd[dp] = fs[dp]
    for g in range(OWN):
        rp[g, me] = sp[me, g]
        rq[g, me] = sq[me, g]
    hx[...] = jnp.zeros_like(hx)
    qh[512:, :] = jnp.zeros((256, HALF), BF16)
    ql[512:, :] = jnp.zeros((256, HALF), BF16)
    over(ND, lambda o: fd_copy(o).wait_recv())
    for s in range(8):
        ft[s] = fd[:, s, :]
    over(NC, lambda o: f_copy(o).start())
    over(NC, lambda o: q_copy(o).start())
    fr[me] = ft[lax.div(me, 2)]
    over(NC, lambda o: f_copy(o).wait_recv())

    lane32 = lax.broadcasted_iota(jnp.int32, (32, HALF), 1)
    odd = lax.rem(me, 2)
    for g in range(OWN):
        total = jnp.zeros((32, HALF), F32)
        for j in range(4):
            part = jnp.concatenate([fr[k, j :: 4, :] for k in range(NC)], axis=0)
            turned = [pltpu.roll(part, (32 * (j - 2 * e - g)) % HALF, axis=1) for e in range(2)]
            part = jnp.where(odd == 1, turned[1], turned[0])
            total = jnp.where((lane32 >= 32 * j) & (lane32 < 32 * j + 32), part, total)
        hx[g, 8:40, :] = total

    row = lax.broadcasted_iota(jnp.int32, (HALF, HALF), 0)
    lane = lax.broadcasted_iota(jnp.int32, (HALF, HALF), 1)
    for g in range(OWN):
        @pl.loop(0, 33)
        def _(q):
            first = jnp.broadcast_to(hx[g, pl.ds(39 - q, 1), :], (HALF, HALF))
            second = jnp.broadcast_to(hx[g, pl.ds(38 - q, 1), :], (HALF, HALF))
            value = jnp.where(lane + row < HALF, first, second)
            high, low = split(pltpu.roll(value, 0, axis=1, stride=1, stride_axis=0))
            rows = pl.ds(pl.multiple_of(q * HALF, HALF), HALF)
            r1h[g, rows, :] = high
            r1l[g, rows, :] = low

    def tile(strip, g, d):
        start = 3968 - 256 * d
        return jnp.concatenate(
            [strip[g, start : start + BLK, :], strip[g, start - HALF : start - HALF + BLK, :]],
            axis=1)

    flip = (row + lane == HALF - 1).astype(BF16)

    over(NC, lambda o: p_copy(o).wait_recv())
    @pl.loop(0, OWN)
    def _(g):
        part_h, part_l = split(rp[g].reshape(512, HALF))
        pth[g] = dot_nt(flip, part_h).astype(BF16)
        ptl[g] = dot_nt(flip, part_l).astype(BF16)
        whole = jnp.concatenate(
            [rp[g, :, 0].reshape(BLK, HALF), rp[g, :, 1].reshape(BLK, HALF)], axis=1)
        xh[...], xl[...] = split(whole)
        for d in range(NC):
            n = (NC - d) * 16
            high, low = tile(r1h, g, d), tile(r1l, g, d)
            value = dot(xh[:n], high) + dot(xl[:n], high) + dot(xh[:n], low)
            value = value.reshape(NC - d, 16, BLK)
            if d == 0:
                yb[g] = value
            else:
                yb[g, d:] += value
        over(NC, lambda o: y_copy(g, o).start())
        cv[me, g] = yb[g, me]

    over(NC, lambda o: q_copy(o).wait_recv())
    @pl.loop(0, OWN)
    def _(g):
        whole = jnp.concatenate(
            [rq[g, :, 0].reshape(BLK, HALF), rq[g, :, 1].reshape(BLK, HALF)], axis=1)
        xh[...], xl[...] = split(whole)
        for d in range(NC):
            high, low = tile(r1h, g, d), tile(r1l, g, d)
            value = dot_nt(xh[d * 16 :], high) + dot_nt(xl[d * 16 :], high) + dot_nt(xh[d * 16 :], low)
            value = value.reshape(NC - d, 16, BLK)
            if d == 0:
                zb[g] = value
            else:
                zb[g, : NC - d] += value
        over(NC, lambda o: z_copy(g, o).start())
        pv[me, g] = zb[g, me]

    below = lane <= row
    fo[...] = jnp.zeros_like(fo)
    lane16 = lax.broadcasted_iota(jnp.int32, (32, HALF), 1)
    s2[...] = jnp.zeros_like(s2)
    for g in range(OWN):
        qh[:512, :], ql[:512, :] = split(rq[g].reshape(512, HALF))
        for e in range(16):
            depth = 512 if e < 8 else 256
            high, low = [
                jnp.concatenate([b[32 * e : 32 * e + depth, :], b[32 * e + 16 : 32 * e + 16 + depth, :]], axis=1)
                for b in (qh, ql)]
            left_h, left_l = pth[g, :, :depth], ptl[g, :, :depth]
            value = dot(left_h, high) + dot(left_l, high) + dot(left_h, low)
            for h in range(2):
                lag = 2 * e + h
                turned = pltpu.roll(value[:, h * HALF : (h + 1) * HALF], 1, axis=1, stride=1, stride_axis=0)
                s1[g, lag : lag + 1, :] = jnp.sum(jnp.where(below, turned, 0.0), axis=0, keepdims=True)
                if lag:
                    s2[g, lag - 1 : lag, :] = jnp.sum(jnp.where(below, 0.0, turned), axis=0, keepdims=True)
    sums = [s1[g] + s2[g] for g in range(OWN)]
    for j in range(4):
        total = jnp.zeros((32, HALF), F32)
        for g in range(OWN):
            for e in range(2):
                turned = pltpu.roll(sums[g], (32 * (2 * e + g - j)) % HALF, axis=1)
                start = 32 * (2 * e + g)
                mask = (lane16 >= start) & (lane16 < start + 32) & (odd == e)
                total = jnp.where(mask, turned, total)
        total = total.reshape(NC, 2, HALF)
        for h in range(2):
            fo[:, 4 * h + j, :] = total[:, h, :]
    over(NC, lambda o: g_copy(o).start())
    fa[me] = fo[me]

    for g in range(OWN):
        over(NC, lambda o: y_copy(g, o).wait_recv())

    @pl.loop(0, NC)
    def _(k):
        rows = pl.ds(pl.multiple_of(k * 32, 32), 32)
        conv = cv[k].reshape(32, BLK)
        mixed[rows, :] = (proj[0, rows, :].astype(F32) * conv).astype(BF16)
        pgrad[0, rows, :] = (cot[rows, :].astype(F32) * conv).astype(BF16)

    over(NC, lambda o: g_copy(o).wait_recv())
    for s in range(8):
        fb[:, s, :] = fa[2 * s] + fa[2 * s + 1]
    over(ND, lambda o: gd_copy(o).start())
    fc[dp] = fb[dp]

    for g in range(OWN):
        over(NC, lambda o: z_copy(g, o).wait_recv())

    @pl.loop(0, NC)
    def _(k):
        rows = pl.ds(pl.multiple_of(k * 32, 32), 32)
        grad = pv[k].reshape(32, BLK)
        pgrad[1, rows, :] = (grad * proj[2, rows, :].astype(F32)).astype(BF16)
        pgrad[2, rows, :] = (grad * proj[1, rows, :].astype(F32)).astype(BF16)

    over(ND, lambda o: gd_copy(o).wait_recv())
    last = fc[...].reshape(64, HALF)
    for q in range(4):
        fgrad[pl.ds(q, 64, stride=4), :] = last[:, 32 * q : 32 * q + 32]

    def finish(o):
        for make in (p_copy, q_copy, f_copy, g_copy):
            make(o).wait_send()
        for g in range(OWN):
            y_copy(g, o).wait_send()
            z_copy(g, o).wait_send()

    over(NC, finish)

    def finish_dp(o):
        fd_copy(o).wait_send()
        gd_copy(o).wait_send()

    over(ND, finish_dp)


def on_device(projected, filters, cotangent):
    rows, cols = cotangent.shape
    vmem = pl.BlockSpec(memory_space=pltpu.VMEM)
    f32 = lambda *shape: pltpu.VMEM(shape, F32)
    b16 = lambda *shape: pltpu.VMEM(shape, BF16)
    strip = (OWN, 33 * HALF, HALF)
    return pl.pallas_call(
        kernel,
        out_shape=(
            jax.ShapeDtypeStruct((rows, cols), BF16),
            jax.ShapeDtypeStruct((3, rows, cols), BF16),
            jax.ShapeDtypeStruct(filters.shape, F32),
        ),
        in_specs=[vmem] * 3,
        out_specs=(vmem,) * 3,
        scratch_shapes=[
            f32(NC, OWN, 2, GROUP, HALF), f32(NC, OWN, 2, GROUP, HALF),
            f32(OWN, NC, 2, GROUP, HALF), f32(OWN, NC, 2, GROUP, HALF),
            f32(OWN, NC, GROUP, BLK), f32(OWN, NC, GROUP, BLK),
            f32(NC, OWN, GROUP, BLK), f32(NC, OWN, GROUP, BLK),
            f32(ND, 8, HALF), f32(ND, 8, HALF), f32(8, ND, HALF), f32(NC, 8, HALF),
            f32(OWN, 40, HALF), b16(*strip), b16(*strip),
            b16(BLK, BLK), b16(BLK, BLK), b16(OWN, HALF, 512), b16(OWN, HALF, 512),
            b16(768, HALF), b16(768, HALF), f32(OWN, 32, HALF), f32(OWN, 32, HALF),
            f32(NC, ND, HALF), f32(NC, ND, HALF), f32(ND, 8, HALF), f32(ND, 8, HALF),
            pltpu.SemaphoreType.DMA((8, NC)), pltpu.SemaphoreType.DMA((8, NC)),
            pltpu.SemaphoreType.DMA((2, ND)), pltpu.SemaphoreType.DMA((2, ND)),
        ],
        compiler_params=pltpu.CompilerParams(
            collective_id=0, has_side_effects=True, vmem_limit_bytes=40 << 20),
    )(projected, filters, cotangent)


def solution(mesh):
    in_specs = (P(None, "dp", "ctx"), P(None, ("ctx", "dp")), P("dp", "ctx"))
    out_specs = (P("dp", "ctx"), P(None, "dp", "ctx"), P(None, ("ctx", "dp")))
    return jax.shard_map(
        on_device, mesh=mesh, in_specs=in_specs, out_specs=out_specs, check_vma=False
    )
```

time: 671 us -> 54.3 us (0.08); the launches traced: 663 us -> 54 us
  waiting for transfers between devices: 488 us -> 0 us
  starting transfers between devices: 59.7 us -> 0 us
  Pallas kernels: 0 us -> 48.2 us
  other arithmetic: 44 us -> 0 us
  matrix products: 43.3 us -> 0 us
  blocking collectives: 13.9 us -> 0 us
    ppermute x48 -> x0, waiting for transfers between devices: 482 us -> none  [from_partner(): return lax.ppermute(value, axis, pairs)]
    ppermute x48 -> x0, starting transfers between devices: 52.2 us -> none  [from_partner(): return lax.ppermute(value, axis, pairs)]
    pallas_call x0 -> x1, Pallas kernels: none -> 48.2 us  [on_device(): pl.pallas_call(kernel, out_shape=(jax.ShapeDtypeStruct((rows, cols), BF16...]
    dot_general x24 -> x0, matrix products: 43.3 us -> none  [exact_dot(): return jnp.dot(left, right, precision=lax.Precision.HIGHEST)]
    mul x17 -> x0, other arithmetic: 19.8 us -> none  [the longest x10 14.5 us: inverse_pairs(): jnp.where(is_upper, first_im - turned_im, first_im + turned_im) * 0.5]
    all_to_all x1 -> x0, blocking collectives: 13.9 us -> none  [on_device(): lax.all_to_all(filter_time, 'dp', split_axis=1, concat_axis=0, tiled=True)]
    select_n x9 -> x0, other arithmetic: 10.5 us -> none  [forward_pairs(): imag_part = jnp.where(is_upper, turned_im, imag_part + other_im)]
    all_to_all x1 -> x0, starting transfers between devices: 7.51 us -> none  [on_device(): lax.all_to_all(filters, 'dp', split_axis=0, concat_axis=1, tiled=True)]
  transfers between devices with their start and end apart: 49 -> 0, of which waited for: 38 -> 0; matrix products, arithmetic and copies ran while one was open for 5% -> 0% of each run, Pallas kernels for 0% -> 0%
where the time goes in v1:
time: 54.3 us; the launch traced here: 54 us
  Pallas kernels  48.2 us (89%)
  local copies, waits for them, and re-layouts  5.21 us (10%)
  between operations  0.65 us (1%)
    pallas_call x1, Pallas kernels, on_device(): pl.pallas_call(kernel, out_shape=(jax.ShapeDtypeStruct((rows, cols), BF16...  48.2 us
    unnamed x7, local copies, waits for them, and re-layouts  4.51 us

profile of v1, /device:TPU:1, one launch (start us, length us, event | category | flops | bytes accessed | tf_op | source)
XLA Modules:
  0.0 54.0 jit_solution(18233278613969318086)
XLA Ops:
  0.6 0.9 %copy.6.filt = f32[256,32]{1,0:T(8,128)S(1)} copy(f32[256,32]{0,1:T(8,128)} %param.4) | data formatting | bytes 65536 | tf_op args[1]
  1.5 0.0 copy-start
  1.5 1.1 %copy-done = bf16[3,512,256]{2,1,0:T(8,128)(2,1)S(1)} copy-done((bf16[3,512,256]{2,1,0:T(8,128)(2,1)S(1)}, bf16[3,512,256]{2,1,0:T(8,128)(2,1)}, u32[]{:S(2)}) %copy-start) | copy-done | bytes 786456
  2.6 0.0 copy-start.1
  2.6 0.9 %copy-done.1 = bf16[512,256]{1,0:T(8,128)(2,1)S(1)} copy-done((bf16[512,256]{1,0:T(8,128)(2,1)S(1)}, bf16[512,256]{1,0:T(8,128)(2,1)}, u32[]{:S(2)}) %copy-start.1) | copy-done | bytes 262168
  3.6 48.2 %shard_map.58 = (bf16[512,256]{1,0:T(8,128)(2,1)S(1)}, bf16[3,512,256]{2,1,0:T(8,128)(2,1)S(1)}, f32[256,32]{1,0:T(8,128)S(1)}) custom-call(bf16[3,512,256]{2,1,0:T(8,128)(2,1)S(1)} %copy-done, f32[256,32]{1,0:T(8,128)S(1)} %copy.6.filt, bf16[512,256]{1,0:T(8,128)(2,1)S(1)} %copy-done.1), custom_call_target="tpu_custom_call" | custom-call | tf_op jit(solution)/shard_map/pallas_call | solution.py:286
  51.8 0.7 %copy.7 = f32[256,32]{0,1:T(8,128)} copy(f32[256,32]{1,0:T(8,128)S(1)} %get-tuple-element.5) | data formatting | bytes 65536 | tf_op jit(solution)/shard_map/pallas_call | solution.py:286
  52.4 0.7 %copy.10 = bf16[512,256]{1,0:T(8,128)(2,1)} copy(bf16[512,256]{1,0:T(8,128)(2,1)S(1)} %get-tuple-element.9) | data formatting | bytes 524288
  53.1 0.9 %copy.11 = bf16[3,512,256]{2,1,0:T(8,128)(2,1)} copy(bf16[3,512,256]{2,1,0:T(8,128)(2,1)S(1)} %get-tuple-element.10) | data formatting | bytes 1572864
Async XLA Ops:
  1.5 1.1 %copy-start = (bf16[3,512,256]{2,1,0:T(8,128)(2,1)S(1)}, bf16[3,512,256]{2,1,0:T(8,128)(2,1)}, u32[]{:S(2)}) copy-start(bf16[3,512,256]{2,1,0:T(8,128)(2,1)} %proj.1) | copy-start | bytes 2359300
  2.6 0.9 %copy-start.1 = (bf16[512,256]{1,0:T(8,128)(2,1)S(1)}, bf16[512,256]{1,0:T(8,128)(2,1)}, u32[]{:S(2)}) copy-start(bf16[512,256]{1,0:T(8,128)(2,1)} %cot.1) | copy-start | bytes 786436

commit v2 on v1

--- a/solution.py
+++ b/solution.py
@@ -33,11 +33,12 @@
 
 
 def kernel(
-    proj, filt, cot, mixed, pgrad, fgrad,
+    proj_in, filt_in, cot_in, mixed, pgrad, fgrad,
+    proj, filt, cot, filt_rows,
     sp, sq, rp, rq, yb, zb, cv, pv,
     fs, fd, ft, fr, hx, r1h, r1l,
     xh, xl, pth, ptl, qh, ql, s1, s2, fo, fa, fb, fc,
-    ssem, rsem, dssem, drsem,
+    ssem, rsem, dssem, drsem, lsem,
 ):
     me = lax.axis_index("ctx")
     dp = lax.axis_index("dp")
@@ -88,16 +89,33 @@
             body(o)
 
     barrier = pltpu.get_barrier_semaphore()
+    over(ND, lambda o: pl.semaphore_signal(
+        barrier, inc=1, device_id=(me, dp_peer(o)), device_id_type=MESH))
     over(NC, lambda o: pl.semaphore_signal(
         barrier, inc=1, device_id=(ctx_peer(o), dp), device_id_type=MESH))
-    over(ND, lambda o: pl.semaphore_signal(
-        barrier, inc=1, device_id=(me, dp_peer(o)), device_id_type=MESH))
+    loads = [
+        pltpu.make_async_copy(filt_in, filt, lsem.at[0]),
+        pltpu.make_async_copy(proj_in, proj, lsem.at[1]),
+        pltpu.make_async_copy(cot_in, cot, lsem.at[2]),
+    ]
+    for load in loads:
+        load.start()
+    hx[...] = jnp.zeros_like(hx)
+    qh[512:, :] = jnp.zeros((256, HALF), BF16)
+    ql[512:, :] = jnp.zeros((256, HALF), BF16)
+    fo[...] = jnp.zeros_like(fo)
+    s2[...] = jnp.zeros_like(s2)
+    loads[0].wait()
+    filt_rows[...] = filt[...].T
 
     fs[...] = jnp.concatenate(
-        [filt[pl.ds(q, 64, stride=4), :] for q in range(4)], axis=1
+        [filt_rows[pl.ds(q, 64, stride=4), :] for q in range(4)], axis=1
     ).reshape(ND, 8, HALF)
 
-    @pl.loop(0, NC)
+    loads[1].wait()
+    loads[2].wait()
+
+    @pl.loop(0, NC, unroll=4)
     def _(k):
         rows = pl.ds(pl.multiple_of(k * 32, 32), 32)
         gate = proj[0, rows, :].astype(F32)
@@ -115,9 +133,6 @@
     for g in range(OWN):
         rp[g, me] = sp[me, g]
         rq[g, me] = sq[me, g]
-    hx[...] = jnp.zeros_like(hx)
-    qh[512:, :] = jnp.zeros((256, HALF), BF16)
-    ql[512:, :] = jnp.zeros((256, HALF), BF16)
     over(ND, lambda o: fd_copy(o).wait_recv())
     for s in range(8):
         ft[s] = fd[:, s, :]
@@ -139,16 +154,17 @@
 
     row = lax.broadcasted_iota(jnp.int32, (HALF, HALF), 0)
     lane = lax.broadcasted_iota(jnp.int32, (HALF, HALF), 1)
-    for g in range(OWN):
-        @pl.loop(0, 33)
-        def _(q):
-            first = jnp.broadcast_to(hx[g, pl.ds(39 - q, 1), :], (HALF, HALF))
-            second = jnp.broadcast_to(hx[g, pl.ds(38 - q, 1), :], (HALF, HALF))
+
+    def build(g):
+        for q in range(32):
+            first = jnp.broadcast_to(hx[g, 39 - q : 40 - q, :], (HALF, HALF))
+            second = jnp.broadcast_to(hx[g, 38 - q : 39 - q, :], (HALF, HALF))
             value = jnp.where(lane + row < HALF, first, second)
             high, low = split(pltpu.roll(value, 0, axis=1, stride=1, stride_axis=0))
-            rows = pl.ds(pl.multiple_of(q * HALF, HALF), HALF)
-            r1h[g, rows, :] = high
-            r1l[g, rows, :] = low
+            r1h[g, q * HALF : (q + 1) * HALF, :] = high
+            r1l[g, q * HALF : (q + 1) * HALF, :] = low
+        r1h[g, 32 * HALF :, :] = jnp.zeros((HALF, HALF), BF16)
+        r1l[g, 32 * HALF :, :] = jnp.zeros((HALF, HALF), BF16)
 
     def tile(strip, g, d):
         start = 3968 - 256 * d
@@ -161,16 +177,15 @@
     over(NC, lambda o: p_copy(o).wait_recv())
     @pl.loop(0, OWN)
     def _(g):
-        part_h, part_l = split(rp[g].reshape(512, HALF))
-        pth[g] = dot_nt(flip, part_h).astype(BF16)
-        ptl[g] = dot_nt(flip, part_l).astype(BF16)
+        build(g)
         whole = jnp.concatenate(
             [rp[g, :, 0].reshape(BLK, HALF), rp[g, :, 1].reshape(BLK, HALF)], axis=1)
         xh[...], xl[...] = split(whole)
         for d in range(NC):
             n = (NC - d) * 16
             high, low = tile(r1h, g, d), tile(r1l, g, d)
-            value = dot(xh[:n], high) + dot(xl[:n], high) + dot(xh[:n], low)
+            both = dot(jnp.concatenate([xh[:n], xl[:n]], axis=0), high)
+            value = both[:n] + both[n:] + dot(xh[:n], low)
             value = value.reshape(NC - d, 16, BLK)
             if d == 0:
                 yb[g] = value
@@ -179,27 +194,15 @@
         over(NC, lambda o: y_copy(g, o).start())
         cv[me, g] = yb[g, me]
 
-    over(NC, lambda o: q_copy(o).wait_recv())
     @pl.loop(0, OWN)
     def _(g):
-        whole = jnp.concatenate(
-            [rq[g, :, 0].reshape(BLK, HALF), rq[g, :, 1].reshape(BLK, HALF)], axis=1)
-        xh[...], xl[...] = split(whole)
-        for d in range(NC):
-            high, low = tile(r1h, g, d), tile(r1l, g, d)
-            value = dot_nt(xh[d * 16 :], high) + dot_nt(xl[d * 16 :], high) + dot_nt(xh[d * 16 :], low)
-            value = value.reshape(NC - d, 16, BLK)
-            if d == 0:
-                zb[g] = value
-            else:
-                zb[g, : NC - d] += value
-        over(NC, lambda o: z_copy(g, o).start())
-        pv[me, g] = zb[g, me]
-
+        part_h, part_l = split(rp[g].reshape(512, HALF))
+        pth[g] = dot_nt(flip, part_h).astype(BF16)
+        ptl[g] = dot_nt(flip, part_l).astype(BF16)
+
+    over(NC, lambda o: q_copy(o).wait_recv())
     below = lane <= row
-    fo[...] = jnp.zeros_like(fo)
     lane16 = lax.broadcasted_iota(jnp.int32, (32, HALF), 1)
-    s2[...] = jnp.zeros_like(s2)
     for g in range(OWN):
         qh[:512, :], ql[:512, :] = split(rq[g].reshape(512, HALF))
         for e in range(16):
@@ -230,15 +233,23 @@
     over(NC, lambda o: g_copy(o).start())
     fa[me] = fo[me]
 
-    for g in range(OWN):
-        over(NC, lambda o: y_copy(g, o).wait_recv())
-
-    @pl.loop(0, NC)
-    def _(k):
-        rows = pl.ds(pl.multiple_of(k * 32, 32), 32)
-        conv = cv[k].reshape(32, BLK)
-        mixed[rows, :] = (proj[0, rows, :].astype(F32) * conv).astype(BF16)
-        pgrad[0, rows, :] = (cot[rows, :].astype(F32) * conv).astype(BF16)
+    @pl.loop(0, OWN)
+    def _(g):
+        whole = jnp.concatenate(
+            [rq[g, :, 0].reshape(BLK, HALF), rq[g, :, 1].reshape(BLK, HALF)], axis=1)
+        xh[...], xl[...] = split(whole)
+        for d in range(NC):
+            n = (NC - d) * 16
+            high, low = tile(r1h, g, d), tile(r1l, g, d)
+            both = dot_nt(jnp.concatenate([xh[d * 16 :], xl[d * 16 :]], axis=0), high)
+            value = both[:n] + both[n:] + dot_nt(xh[d * 16 :], low)
+            value = value.reshape(NC - d, 16, BLK)
+            if d == 0:
+                zb[g] = value
+            else:
+                zb[g, : NC - d] += value
+        over(NC, lambda o: z_copy(g, o).start())
+        pv[me, g] = zb[g, me]
 
     over(NC, lambda o: g_copy(o).wait_recv())
     for s in range(8):
@@ -246,20 +257,43 @@
     over(ND, lambda o: gd_copy(o).start())
     fc[dp] = fb[dp]
 
-    for g in range(OWN):
-        over(NC, lambda o: z_copy(g, o).wait_recv())
-
-    @pl.loop(0, NC)
-    def _(k):
+    def gate_block(k):
+        rows = pl.ds(pl.multiple_of(k * 32, 32), 32)
+        conv = cv[k].reshape(32, BLK)
+        mixed[rows, :] = (proj[0, rows, :].astype(F32) * conv).astype(BF16)
+        pgrad[0, rows, :] = (cot[rows, :].astype(F32) * conv).astype(BF16)
+
+    def value_block(k):
         rows = pl.ds(pl.multiple_of(k * 32, 32), 32)
         grad = pv[k].reshape(32, BLK)
         pgrad[1, rows, :] = (grad * proj[2, rows, :].astype(F32)).astype(BF16)
         pgrad[2, rows, :] = (grad * proj[1, rows, :].astype(F32)).astype(BF16)
 
+    def ctx_source(o):
+        return lax.rem(me + NC - o, NC)
+
+    gate_block(me)
+
+    def take_conv(o):
+        for g in range(OWN):
+            y_copy(g, o).wait_recv()
+        gate_block(ctx_source(o))
+
+    over(NC, take_conv)
+    value_block(me)
+
+    def take_grad(o):
+        for g in range(OWN):
+            z_copy(g, o).wait_recv()
+        value_block(ctx_source(o))
+
+    over(NC, take_grad)
+
     over(ND, lambda o: gd_copy(o).wait_recv())
     last = fc[...].reshape(64, HALF)
     for q in range(4):
-        fgrad[pl.ds(q, 64, stride=4), :] = last[:, 32 * q : 32 * q + 32]
+        filt_rows[pl.ds(q, 64, stride=4), :] = last[:, 32 * q : 32 * q + 32]
+    fgrad[...] = filt_rows[...].T
 
     def finish(o):
         for make in (p_copy, q_copy, f_copy, g_copy):
@@ -283,16 +317,18 @@
     f32 = lambda *shape: pltpu.VMEM(shape, F32)
     b16 = lambda *shape: pltpu.VMEM(shape, BF16)
     strip = (OWN, 33 * HALF, HALF)
-    return pl.pallas_call(
+    whole = pl.BlockSpec(memory_space=pl.ANY)
+    mixed, proj_grad, filter_grad = pl.pallas_call(
         kernel,
         out_shape=(
             jax.ShapeDtypeStruct((rows, cols), BF16),
             jax.ShapeDtypeStruct((3, rows, cols), BF16),
-            jax.ShapeDtypeStruct(filters.shape, F32),
+            jax.ShapeDtypeStruct(filters.shape[::-1], F32),
         ),
-        in_specs=[vmem] * 3,
+        in_specs=[whole] * 3,
         out_specs=(vmem,) * 3,
         scratch_shapes=[
+            b16(3, rows, cols), f32(*filters.shape[::-1]), b16(rows, cols), f32(*filters.shape),
             f32(NC, OWN, 2, GROUP, HALF), f32(NC, OWN, 2, GROUP, HALF),
             f32(OWN, NC, 2, GROUP, HALF), f32(OWN, NC, 2, GROUP, HALF),
             f32(OWN, NC, GROUP, BLK), f32(OWN, NC, GROUP, BLK),
@@ -303,11 +339,12 @@
             b16(768, HALF), b16(768, HALF), f32(OWN, 32, HALF), f32(OWN, 32, HALF),
             f32(NC, ND, HALF), f32(NC, ND, HALF), f32(ND, 8, HALF), f32(ND, 8, HALF),
             pltpu.SemaphoreType.DMA((8, NC)), pltpu.SemaphoreType.DMA((8, NC)),
-            pltpu.SemaphoreType.DMA((2, ND)), pltpu.SemaphoreType.DMA((2, ND)),
+            pltpu.SemaphoreType.DMA((2, ND)), pltpu.SemaphoreType.DMA((2, ND)), pltpu.SemaphoreType.DMA((3,)),
         ],
         compiler_params=pltpu.CompilerParams(
-            collective_id=0, has_side_effects=True, vmem_limit_bytes=40 << 20),
-    )(projected, filters, cotangent)
+            collective_id=0, has_side_effects=True, vmem_limit_bytes=56 << 20),
+    )(projected, filters.T, cotangent)
+    return mixed, proj_grad, filter_grad.T
 
 
 def solution(mesh):

time: 54.3 us -> 46.7 us (0.86)
  Pallas kernels: 48.2 us -> 41.5 us
  local copies, waits for them, and re-layouts: 5.21 us -> 4.36 us
    pallas_call x1, Pallas kernels: 48.2 us -> 41.5 us  [on_device(): pl.pallas_call(kernel, out_shape=(jax.ShapeDtypeStruct((rows, cols), BF16...]
    pallas_call x1 -> x0, local copies, waits for them, and re-layouts: 0.69 us -> none  [on_device(): pl.pallas_call(kernel, out_shape=(jax.ShapeDtypeStruct((rows, cols), BF16...]
    unnamed x7 -> x5, local copies, waits for them, and re-layouts: 4.51 us -> 4.36 us
where the time goes in v2:
time: 46.7 us; the launch traced here: 46.5 us
  Pallas kernels  41.5 us (89%)
  local copies, waits for them, and re-layouts  4.36 us (9%)
  between operations  0.64 us (1%)
    pallas_call x1, Pallas kernels, on_device(): pl.pallas_call(kernel, out_shape=(jax.ShapeDtypeStruct((rows, cols), BF16...  41.5 us
    unnamed x5, local copies, waits for them, and re-layouts  4.36 us

profile of v2, /device:TPU:1, one launch (start us, length us, event | category | flops | bytes accessed | tf_op | source)
XLA Modules:
  0.0 46.5 jit_solution(10443166298695103301)
XLA Ops:
  0.6 41.5 %shard_map.58 = (bf16[512,256]{1,0:T(8,128)(2,1)}, bf16[3,512,256]{2,1,0:T(8,128)(2,1)}, f32[32,256]{1,0:T(8,128)}) custom-call(bf16[3,512,256]{2,1,0:T(8,128)(2,1)} %proj_in.1, f32[32,256]{1,0:T(8,128)} %bitcast.2, bf16[512,256]{1,0:T(8,128)(2,1)} %cot_in.1), custom_call_target="tpu_custom_call" | custom-call | tf_op jit(solution)/shard_map/pallas_call | solution.py:321
  42.1 1.7 %copy.9 = bf16[512,256]{1,0:T(8,128)(2,1)} copy(bf16[512,256]{1,0:T(8,128)(2,1)} %get-tuple-element.12) | data formatting | bytes 524288
  43.8 0.0 copy-start
  43.8 2.1 %copy.10 = bf16[3,512,256]{2,1,0:T(8,128)(2,1)} copy(bf16[3,512,256]{2,1,0:T(8,128)(2,1)} %get-tuple-element.13) | data formatting | bytes 1572864
  45.9 0.0 copy-done
  45.9 0.6 %copy.11 = f32[256,32]{0,1:T(8,128)} copy(f32[256,32]{0,1:T(8,128)S(1)} %bitcast.3) | data formatting | bytes 65536
Async XLA Ops:
  43.8 2.1 %copy-start = (f32[32,256]{1,0:T(8,128)S(1)}, f32[32,256]{1,0:T(8,128)}, u32[]{:S(2)}) copy-start(f32[32,256]{1,0:T(8,128)} %get-tuple-element.8) | copy-start | bytes 98308

commit v3 on v2

--- a/solution.py
+++ b/solution.py
@@ -38,7 +38,7 @@
     sp, sq, rp, rq, yb, zb, cv, pv,
     fs, fd, ft, fr, hx, r1h, r1l,
     xh, xl, pth, ptl, qh, ql, s1, s2, fo, fa, fb, fc,
-    ssem, rsem, dssem, drsem, lsem,
+    ssem, rsem, lsem,
 ):
     me = lax.axis_index("ctx")
     dp = lax.axis_index("dp")
@@ -51,12 +51,12 @@
 
     def ctx_copy(kind, o, src, dst):
         return pltpu.make_async_remote_copy(
-            src_ref=src, dst_ref=dst, send_sem=ssem.at[kind, o], recv_sem=rsem.at[kind, o],
+            src_ref=src, dst_ref=dst, send_sem=ssem.at[kind], recv_sem=rsem.at[kind],
             device_id=(ctx_peer(o), dp), device_id_type=MESH)
 
     def dp_copy(kind, o, src, dst):
         return pltpu.make_async_remote_copy(
-            src_ref=src, dst_ref=dst, send_sem=dssem.at[kind, o], recv_sem=drsem.at[kind, o],
+            src_ref=src, dst_ref=dst, send_sem=ssem.at[8 + kind], recv_sem=rsem.at[8 + kind],
             device_id=(me, dp_peer(o)), device_id_type=MESH)
 
     def p_copy(o):
@@ -82,6 +82,20 @@
 
     def gd_copy(o):
         return dp_copy(1, o, fb.at[dp_peer(o)], fc.at[dp])
+
+    totals = [
+        rp.at[:, pl.ds(0, NC - 1)], rq.at[:, pl.ds(0, NC - 1)],
+        cv.at[pl.ds(0, NC - 1), 0], cv.at[pl.ds(0, NC - 1), 1],
+        pv.at[pl.ds(0, NC - 1), 0], pv.at[pl.ds(0, NC - 1), 1],
+        fr.at[pl.ds(0, NC - 1)], fa.at[pl.ds(0, NC - 1)],
+        fd.at[pl.ds(0, ND - 1)], fc.at[pl.ds(0, ND - 1)],
+    ]
+
+    def arrived(kind):
+        pltpu.make_async_copy(totals[kind], totals[kind], rsem.at[kind]).wait()
+
+    def sent(kind):
+        pltpu.make_async_copy(totals[kind], totals[kind], ssem.at[kind]).wait()
 
     def over(n, body):
         @pl.loop(1, n)
@@ -133,13 +147,13 @@
     for g in range(OWN):
         rp[g, me] = sp[me, g]
         rq[g, me] = sq[me, g]
-    over(ND, lambda o: fd_copy(o).wait_recv())
+    arrived(8)
     for s in range(8):
         ft[s] = fd[:, s, :]
     over(NC, lambda o: f_copy(o).start())
     over(NC, lambda o: q_copy(o).start())
     fr[me] = ft[lax.div(me, 2)]
-    over(NC, lambda o: f_copy(o).wait_recv())
+    arrived(6)
 
     lane32 = lax.broadcasted_iota(jnp.int32, (32, HALF), 1)
     odd = lax.rem(me, 2)
@@ -174,7 +188,7 @@
 
     flip = (row + lane == HALF - 1).astype(BF16)
 
-    over(NC, lambda o: p_copy(o).wait_recv())
+    arrived(0)
     @pl.loop(0, OWN)
     def _(g):
         build(g)
@@ -200,7 +214,7 @@
         pth[g] = dot_nt(flip, part_h).astype(BF16)
         ptl[g] = dot_nt(flip, part_l).astype(BF16)
 
-    over(NC, lambda o: q_copy(o).wait_recv())
+    arrived(1)
     below = lane <= row
     lane16 = lax.broadcasted_iota(jnp.int32, (32, HALF), 1)
     for g in range(OWN):
@@ -251,64 +265,49 @@
         over(NC, lambda o: z_copy(g, o).start())
         pv[me, g] = zb[g, me]
 
-    over(NC, lambda o: g_copy(o).wait_recv())
+    arrived(7)
     for s in range(8):
         fb[:, s, :] = fa[2 * s] + fa[2 * s + 1]
     over(ND, lambda o: gd_copy(o).start())
     fc[dp] = fb[dp]
 
-    def gate_block(k):
+    arrived(2)
+    arrived(3)
+
+    @pl.loop(0, NC, unroll=4)
+    def _(k):
         rows = pl.ds(pl.multiple_of(k * 32, 32), 32)
         conv = cv[k].reshape(32, BLK)
         mixed[rows, :] = (proj[0, rows, :].astype(F32) * conv).astype(BF16)
         pgrad[0, rows, :] = (cot[rows, :].astype(F32) * conv).astype(BF16)
 
-    def value_block(k):
-        rows = pl.ds(pl.multiple_of(k * 32, 32), 32)
-        grad = pv[k].reshape(32, BLK)
-        pgrad[1, rows, :] = (grad * proj[2, rows, :].astype(F32)).astype(BF16)
-        pgrad[2, rows, :] = (grad * proj[1, rows, :].astype(F32)).astype(BF16)
-
-    def ctx_source(o):
-        return lax.rem(me + NC - o, NC)
-
-    gate_block(me)
-
-    def take_conv(o):
-        for g in range(OWN):
-            y_copy(g, o).wait_recv()
-        gate_block(ctx_source(o))
-
-    over(NC, take_conv)
-    value_block(me)
-
-    def take_grad(o):
-        for g in range(OWN):
-            z_copy(g, o).wait_recv()
-        value_block(ctx_source(o))
-
-    over(NC, take_grad)
-
-    over(ND, lambda o: gd_copy(o).wait_recv())
+    for g in range(OWN):
+        arrived(4 + g)
+
+        @pl.loop(0, NC, unroll=4)
+        def _(k):
+            rows = pl.ds(pl.multiple_of(k * 32 + g * 16, 16), 16)
+            grad = pv[k, g]
+            pgrad[1, rows, :] = (grad * proj[2, rows, :].astype(F32)).astype(BF16)
+            pgrad[2, rows, :] = (grad * proj[1, rows, :].astype(F32)).astype(BF16)
+
+    arrived(9)
     last = fc[...].reshape(64, HALF)
     for q in range(4):
         filt_rows[pl.ds(q, 64, stride=4), :] = last[:, 32 * q : 32 * q + 32]
     fgrad[...] = filt_rows[...].T
 
-    def finish(o):
-        for make in (p_copy, q_copy, f_copy, g_copy):
-            make(o).wait_send()
-        for g in range(OWN):
-            y_copy(g, o).wait_send()
-            z_copy(g, o).wait_send()
-
-    over(NC, finish)
-
-    def finish_dp(o):
-        fd_copy(o).wait_send()
-        gd_copy(o).wait_send()
-
-    over(ND, finish_dp)
+    for kind in range(10):
+        sent(kind)
+
+
+def write_out(mixed, pgrad, fgrad, mixed_out, pgrad_out, fgrad_out, sem):
+    pairs = [(mixed, mixed_out), (pgrad, pgrad_out), (fgrad, fgrad_out)]
+    copies = [pltpu.make_async_copy(a, b, sem.at[i]) for i, (a, b) in enumerate(pairs)]
+    for copy in copies:
+        copy.start()
+    for copy in copies:
+        copy.wait()
 
 
 def on_device(projected, filters, cotangent):
@@ -317,7 +316,7 @@
     f32 = lambda *shape: pltpu.VMEM(shape, F32)
     b16 = lambda *shape: pltpu.VMEM(shape, BF16)
     strip = (OWN, 33 * HALF, HALF)
-    whole = pl.BlockSpec(memory_space=pl.ANY)
+    whole = pl.BlockSpec(memory_space=pltpu.HBM)
     mixed, proj_grad, filter_grad = pl.pallas_call(
         kernel,
         out_shape=(
@@ -338,13 +337,20 @@
             b16(BLK, BLK), b16(BLK, BLK), b16(OWN, HALF, 512), b16(OWN, HALF, 512),
             b16(768, HALF), b16(768, HALF), f32(OWN, 32, HALF), f32(OWN, 32, HALF),
             f32(NC, ND, HALF), f32(NC, ND, HALF), f32(ND, 8, HALF), f32(ND, 8, HALF),
-            pltpu.SemaphoreType.DMA((8, NC)), pltpu.SemaphoreType.DMA((8, NC)),
-            pltpu.SemaphoreType.DMA((2, ND)), pltpu.SemaphoreType.DMA((2, ND)), pltpu.SemaphoreType.DMA((3,)),
+            pltpu.SemaphoreType.DMA((10,)), pltpu.SemaphoreType.DMA((10,)), pltpu.SemaphoreType.DMA((3,)),
         ],
         compiler_params=pltpu.CompilerParams(
-            collective_id=0, has_side_effects=True, vmem_limit_bytes=56 << 20),
-    )(projected, filters.T, cotangent)
-    return mixed, proj_grad, filter_grad.T
+            collective_id=0, has_side_effects=True, vmem_limit_bytes=48 << 20),
+    )(*[pltpu.with_memory_space_constraint(x, pltpu.HBM) for x in (projected, filters.T, cotangent)])
+    parts = [pltpu.with_memory_space_constraint(x, pltpu.VMEM) for x in (mixed, proj_grad, filter_grad)]
+    results = pl.pallas_call(
+        write_out,
+        out_shape=[jax.ShapeDtypeStruct(x.shape, x.dtype) for x in (mixed, proj_grad, filter_grad)],
+        in_specs=[vmem] * 3,
+        out_specs=[pl.BlockSpec(memory_space=pl.ANY)] * 3,
+        scratch_shapes=[pltpu.SemaphoreType.DMA((3,))],
+    )(*parts)
+    return results[0], results[1], results[2].T
 
 
 def solution(mesh):

time: 46.7 us -> 39.5 us (0.85)
  local copies, waits for them, and re-layouts: 4.36 us -> 0 us
  Pallas kernels: 41.5 us -> 38.7 us
    unnamed x5 -> x0, local copies, waits for them, and re-layouts: 4.36 us -> none
    pallas_call x1, Pallas kernels: 41.5 us -> 37.8 us  [on_device(): pl.pallas_call(kernel, out_shape=(jax.ShapeDtypeStruct((rows, cols), BF16...]
    pallas_call x0 -> x1, Pallas kernels: none -> 1 us  [on_device(): pl.pallas_call(write_out, out_shape=[jax.ShapeDtypeStruct(x.shape, x.dtyp...]
where the time goes in v3:
time: 39.5 us; the launch traced here: 39.4 us
  Pallas kernels  38.7 us (98%)
  between operations  0.64 us (2%)
    pallas_call x1, Pallas kernels, on_device(): pl.pallas_call(kernel, out_shape=(jax.ShapeDtypeStruct((rows, cols), BF16...  37.8 us
    pallas_call x1, Pallas kernels, on_device(): pl.pallas_call(write_out, out_shape=[jax.ShapeDtypeStruct(x.shape, x.dtyp...  1 us

profile of v3, /device:TPU:1, one launch (start us, length us, event | category | flops | bytes accessed | tf_op | source)
XLA Modules:
  0.0 39.4 jit_solution(14786917624143249685)
XLA Ops:
  0.6 37.8 %shard_map.58 = (bf16[512,256]{1,0:T(8,128)(2,1)S(1)}, bf16[3,512,256]{2,1,0:T(8,128)(2,1)S(1)}, f32[32,256]{1,0:T(8,128)S(1)}) custom-call(bf16[3,512,256]{2,1,0:T(8,128)(2,1)} %proj_in.1, f32[32,256]{1,0:T(8,128)} %bitcast.2, bf16[512,256]{1,0:T(8,128)(2,1)} %cot_in.1), custom_call_target="tpu_custom_call" | custom-call | tf_op jit(solution)/shard_map/pallas_call | solution.py:320
  38.4 1.0 %shard_map.59 = (bf16[512,256]{1,0:T(8,128)(2,1)}, bf16[3,512,256]{2,1,0:T(8,128)(2,1)}, f32[32,256]{1,0:T(8,128)}) custom-call(bf16[512,256]{1,0:T(8,128)(2,1)S(1)} %get-tuple-element.9.mixed, bf16[3,512,256]{2,1,0:T(8,128)(2,1)S(1)} %get-tuple-element.10.pgrad, f32[32,256]{1,0:T(8,128)S(1)} %get-tuple-element.11.fgrad), custom_call_target="tpu_custom_call" | custom-call | tf_op jit(solution)/shard_map/pallas_call | solution.py:346

commit v4 on v3

--- a/solution.py
+++ b/solution.py
@@ -62,8 +62,8 @@
     def p_copy(o):
         return ctx_copy(0, o, sp.at[ctx_peer(o)], rp.at[:, me])
 
-    def q_copy(o):
-        return ctx_copy(1, o, sq.at[ctx_peer(o)], rq.at[:, me])
+    def q_copy(g, o):
+        return ctx_copy(1 if g == 0 else 10, o, sq.at[ctx_peer(o), g], rq.at[g, me])
 
     def y_copy(g, o):
         return ctx_copy(2 + g, o, yb.at[g, ctx_peer(o)], cv.at[me, g])
@@ -84,11 +84,11 @@
         return dp_copy(1, o, fb.at[dp_peer(o)], fc.at[dp])
 
     totals = [
-        rp.at[:, pl.ds(0, NC - 1)], rq.at[:, pl.ds(0, NC - 1)],
+        rp.at[:, pl.ds(0, NC - 1)], rq.at[0, pl.ds(0, NC - 1)],
         cv.at[pl.ds(0, NC - 1), 0], cv.at[pl.ds(0, NC - 1), 1],
         pv.at[pl.ds(0, NC - 1), 0], pv.at[pl.ds(0, NC - 1), 1],
         fr.at[pl.ds(0, NC - 1)], fa.at[pl.ds(0, NC - 1)],
-        fd.at[pl.ds(0, ND - 1)], fc.at[pl.ds(0, ND - 1)],
+        fd.at[pl.ds(0, ND - 1)], fc.at[pl.ds(0, ND - 1)], rq.at[1, pl.ds(0, NC - 1)],
     ]
 
     def arrived(kind):
@@ -103,55 +103,75 @@
             body(o)
 
     barrier = pltpu.get_barrier_semaphore()
-    over(ND, lambda o: pl.semaphore_signal(
-        barrier, inc=1, device_id=(me, dp_peer(o)), device_id_type=MESH))
-    over(NC, lambda o: pl.semaphore_signal(
-        barrier, inc=1, device_id=(ctx_peer(o), dp), device_id_type=MESH))
+    for o in (6, 2, 5, 7, 1, 3, 4):
+        pl.semaphore_signal(barrier, inc=1, device_id=(me, dp_peer(o)), device_id_type=MESH)
+    for o in range(1, NC):
+        pl.semaphore_signal(barrier, inc=1, device_id=(ctx_peer(o), dp), device_id_type=MESH)
     loads = [
         pltpu.make_async_copy(filt_in, filt, lsem.at[0]),
-        pltpu.make_async_copy(proj_in, proj, lsem.at[1]),
-        pltpu.make_async_copy(cot_in, cot, lsem.at[2]),
+        pltpu.make_async_copy(proj_in.at[pl.ds(1, 2)], proj.at[pl.ds(1, 2)], lsem.at[1]),
+        pltpu.make_async_copy(proj_in.at[0], proj.at[0], lsem.at[2]),
+        pltpu.make_async_copy(cot_in, cot, lsem.at[3]),
     ]
     for load in loads:
         load.start()
+    loads[0].wait()
+    filt_rows[...] = filt[...].T
+    fs[...] = jnp.concatenate(
+        [filt_rows[pl.ds(q, 64, stride=4), :] for q in range(4)], axis=1
+    ).reshape(ND, 8, HALF)
+
+    def block(k):
+        return pl.ds(pl.multiple_of(k * 32, 32), 32)
+
+    def product(k):
+        return proj[1, block(k), :].astype(F32) * proj[2, block(k), :].astype(F32)
+
+    def conv_cot(k):
+        return cot[block(k), :].astype(F32) * proj[0, block(k), :].astype(F32)
+
+    def pieces(value):
+        for g in range(OWN):
+            for h in range(2):
+                yield g, h, value[g * 16 : g * 16 + 16, h * HALF : (h + 1) * HALF]
+
+    pl.semaphore_wait(barrier, NC + ND - 2)
+    for o in (6, 2, 5, 7, 1, 3, 4):
+        fd_copy(o).start()
+    loads[1].wait()
+
+    def give_product(o):
+        k = ctx_peer(o)
+        for g, h, piece in pieces(product(k)):
+            sp[k, g, h] = piece
+        p_copy(o).start()
+
+    over(NC, give_product)
+    fd[dp] = fs[dp]
+    for g, h, piece in pieces(product(me)):
+        rp[g, me, h] = piece
+    loads[2].wait()
+    loads[3].wait()
+    for g, h, piece in pieces(conv_cot(me)):
+        rq[g, me, h] = piece
+
+    @pl.loop(0, NC, unroll=4)
+    def _(k):
+        for g, h, piece in pieces(conv_cot(k)):
+            sq[k, g, h] = piece
+
     hx[...] = jnp.zeros_like(hx)
     qh[512:, :] = jnp.zeros((256, HALF), BF16)
     ql[512:, :] = jnp.zeros((256, HALF), BF16)
     fo[...] = jnp.zeros_like(fo)
     s2[...] = jnp.zeros_like(s2)
-    loads[0].wait()
-    filt_rows[...] = filt[...].T
-
-    fs[...] = jnp.concatenate(
-        [filt_rows[pl.ds(q, 64, stride=4), :] for q in range(4)], axis=1
-    ).reshape(ND, 8, HALF)
-
-    loads[1].wait()
-    loads[2].wait()
-
-    @pl.loop(0, NC, unroll=4)
-    def _(k):
-        rows = pl.ds(pl.multiple_of(k * 32, 32), 32)
-        gate = proj[0, rows, :].astype(F32)
-        prod = proj[1, rows, :].astype(F32) * proj[2, rows, :].astype(F32)
-        ccot = cot[rows, :].astype(F32) * gate
-        for g in range(OWN):
-            for h in range(2):
-                sp[k, g, h] = prod[g * 16 : g * 16 + 16, h * HALF : (h + 1) * HALF]
-                sq[k, g, h] = ccot[g * 16 : g * 16 + 16, h * HALF : (h + 1) * HALF]
-
-    pl.semaphore_wait(barrier, NC + ND - 2)
-    over(ND, lambda o: fd_copy(o).start())
-    over(NC, lambda o: p_copy(o).start())
-    fd[dp] = fs[dp]
-    for g in range(OWN):
-        rp[g, me] = sp[me, g]
-        rq[g, me] = sq[me, g]
     arrived(8)
     for s in range(8):
         ft[s] = fd[:, s, :]
-    over(NC, lambda o: f_copy(o).start())
-    over(NC, lambda o: q_copy(o).start())
+    for o in range(1, NC):
+        f_copy(o).start()
+    for g in range(OWN):
+        over(NC, lambda o: q_copy(g, o).start())
     fr[me] = ft[lax.div(me, 2)]
     arrived(6)
 
@@ -214,10 +234,9 @@
         pth[g] = dot_nt(flip, part_h).astype(BF16)
         ptl[g] = dot_nt(flip, part_l).astype(BF16)
 
-    arrived(1)
     below = lane <= row
     lane16 = lax.broadcasted_iota(jnp.int32, (32, HALF), 1)
-    for g in range(OWN):
+    def lag_sums(g):
         qh[:512, :], ql[:512, :] = split(rq[g].reshape(512, HALF))
         for e in range(16):
             depth = 512 if e < 8 else 256
@@ -232,23 +251,7 @@
                 s1[g, lag : lag + 1, :] = jnp.sum(jnp.where(below, turned, 0.0), axis=0, keepdims=True)
                 if lag:
                     s2[g, lag - 1 : lag, :] = jnp.sum(jnp.where(below, 0.0, turned), axis=0, keepdims=True)
-    sums = [s1[g] + s2[g] for g in range(OWN)]
-    for j in range(4):
-        total = jnp.zeros((32, HALF), F32)
-        for g in range(OWN):
-            for e in range(2):
-                turned = pltpu.roll(sums[g], (32 * (2 * e + g - j)) % HALF, axis=1)
-                start = 32 * (2 * e + g)
-                mask = (lane16 >= start) & (lane16 < start + 32) & (odd == e)
-                total = jnp.where(mask, turned, total)
-        total = total.reshape(NC, 2, HALF)
-        for h in range(2):
-            fo[:, 4 * h + j, :] = total[:, h, :]
-    over(NC, lambda o: g_copy(o).start())
-    fa[me] = fo[me]
-
-    @pl.loop(0, OWN)
-    def _(g):
+    def correlate(g):
         whole = jnp.concatenate(
             [rq[g, :, 0].reshape(BLK, HALF), rq[g, :, 1].reshape(BLK, HALF)], axis=1)
         xh[...], xl[...] = split(whole)
@@ -265,10 +268,34 @@
         over(NC, lambda o: z_copy(g, o).start())
         pv[me, g] = zb[g, me]
 
+    arrived(1)
+    lag_sums(0)
+    correlate(0)
+    arrived(10)
+    lag_sums(1)
+    sums = [s1[g] + s2[g] for g in range(OWN)]
+    for j in range(4):
+        total = jnp.zeros((32, HALF), F32)
+        for g in range(OWN):
+            for e in range(2):
+                turned = pltpu.roll(sums[g], (32 * (2 * e + g - j)) % HALF, axis=1)
+                start = 32 * (2 * e + g)
+                mask = (lane16 >= start) & (lane16 < start + 32) & (odd == e)
+                total = jnp.where(mask, turned, total)
+        total = total.reshape(NC, 2, HALF)
+        for h in range(2):
+            fo[:, 4 * h + j, :] = total[:, h, :]
+    for o in range(1, NC):
+        g_copy(o).start()
+    fa[me] = fo[me]
+
+    correlate(1)
+
     arrived(7)
     for s in range(8):
         fb[:, s, :] = fa[2 * s] + fa[2 * s + 1]
-    over(ND, lambda o: gd_copy(o).start())
+    for o in (6, 2, 5, 7, 1, 3, 4):
+        gd_copy(o).start()
     fc[dp] = fb[dp]
 
     arrived(2)
@@ -297,7 +324,7 @@
         filt_rows[pl.ds(q, 64, stride=4), :] = last[:, 32 * q : 32 * q + 32]
     fgrad[...] = filt_rows[...].T
 
-    for kind in range(10):
+    for kind in range(11):
         sent(kind)
 
 
@@ -337,7 +364,7 @@
             b16(BLK, BLK), b16(BLK, BLK), b16(OWN, HALF, 512), b16(OWN, HALF, 512),
             b16(768, HALF), b16(768, HALF), f32(OWN, 32, HALF), f32(OWN, 32, HALF),
             f32(NC, ND, HALF), f32(NC, ND, HALF), f32(ND, 8, HALF), f32(ND, 8, HALF),
-            pltpu.SemaphoreType.DMA((10,)), pltpu.SemaphoreType.DMA((10,)), pltpu.SemaphoreType.DMA((3,)),
+            pltpu.SemaphoreType.DMA((11,)), pltpu.SemaphoreType.DMA((11,)), pltpu.SemaphoreType.DMA((4,)),
         ],
         compiler_params=pltpu.CompilerParams(
             collective_id=0, has_side_effects=True, vmem_limit_bytes=48 << 20),

time: 39.5 us -> 39.1 us (0.990)
  no operation moved by 1% of the time
where the time goes in v4:
time: 39.1 us; the launch traced here: 39 us
  Pallas kernels  38.4 us (98%)
  between operations  0.64 us (2%)
    pallas_call x1, Pallas kernels, on_device(): pl.pallas_call(kernel, out_shape=(jax.ShapeDtypeStruct((rows, cols), BF16...  37.4 us
    pallas_call x1, Pallas kernels, on_device(): pl.pallas_call(write_out, out_shape=[jax.ShapeDtypeStruct(x.shape, x.dtyp...  1 us

profile of v4, /device:TPU:1, one launch (start us, length us, event | category | flops | bytes accessed | tf_op | source)
XLA Modules:
  0.0 39.0 jit_solution(14351908933732863826)
XLA Ops:
  0.6 37.4 %shard_map.58 = (bf16[512,256]{1,0:T(8,128)(2,1)S(1)}, bf16[3,512,256]{2,1,0:T(8,128)(2,1)S(1)}, f32[32,256]{1,0:T(8,128)S(1)}) custom-call(bf16[3,512,256]{2,1,0:T(8,128)(2,1)} %proj_in.1, f32[32,256]{1,0:T(8,128)} %bitcast.2, bf16[512,256]{1,0:T(8,128)(2,1)} %cot_in.1), custom_call_target="tpu_custom_call" | custom-call | tf_op jit(solution)/shard_map/pallas_call | solution.py:347
  38.0 1.0 %shard_map.59 = (bf16[512,256]{1,0:T(8,128)(2,1)}, bf16[3,512,256]{2,1,0:T(8,128)(2,1)}, f32[32,256]{1,0:T(8,128)}) custom-call(bf16[512,256]{1,0:T(8,128)(2,1)S(1)} %get-tuple-element.9.mixed, bf16[3,512,256]{2,1,0:T(8,128)(2,1)S(1)} %get-tuple-element.10.pgrad, f32[32,256]{1,0:T(8,128)S(1)} %get-tuple-element.11.fgrad), custom_call_target="tpu_custom_call" | custom-call | tf_op jit(solution)/shard_map/pallas_call | solution.py:373

commit v5 on v4

--- a/solution.py
+++ b/solution.py
@@ -135,18 +135,17 @@
             for h in range(2):
                 yield g, h, value[g * 16 : g * 16 + 16, h * HALF : (h + 1) * HALF]
 
+    loads[1].wait()
+
+    @pl.loop(0, NC, unroll=4)
+    def _(k):
+        for g, h, piece in pieces(product(k)):
+            sp[k, g, h] = piece
+
     pl.semaphore_wait(barrier, NC + ND - 2)
     for o in (6, 2, 5, 7, 1, 3, 4):
         fd_copy(o).start()
-    loads[1].wait()
-
-    def give_product(o):
-        k = ctx_peer(o)
-        for g, h, piece in pieces(product(k)):
-            sp[k, g, h] = piece
-        p_copy(o).start()
-
-    over(NC, give_product)
+    over(NC, lambda o: p_copy(o).start())
     fd[dp] = fs[dp]
     for g, h, piece in pieces(product(me)):
         rp[g, me, h] = piece

time: 39.1 us -> 39.1 us (level)
  no operation moved by 1% of the time
where the time goes in v5:
time: 39.1 us; the launch traced here: 39 us
  Pallas kernels  38.4 us (98%)
  between operations  0.64 us (2%)
    pallas_call x1, Pallas kernels, on_device(): pl.pallas_call(kernel, out_shape=(jax.ShapeDtypeStruct((rows, cols), BF16...  37.4 us
    pallas_call x1, Pallas kernels, on_device(): pl.pallas_call(write_out, out_shape=[jax.ShapeDtypeStruct(x.shape, x.dtyp...  1 us

profile of v5, /device:TPU:1, one launch (start us, length us, event | category | flops | bytes accessed | tf_op | source)
XLA Modules:
  0.0 39.0 jit_solution(16405465149415683228)
XLA Ops:
  0.6 37.4 %shard_map.58 = (bf16[512,256]{1,0:T(8,128)(2,1)S(1)}, bf16[3,512,256]{2,1,0:T(8,128)(2,1)S(1)}, f32[32,256]{1,0:T(8,128)S(1)}) custom-call(bf16[3,512,256]{2,1,0:T(8,128)(2,1)} %proj_in.1, f32[32,256]{1,0:T(8,128)} %bitcast.2, bf16[512,256]{1,0:T(8,128)(2,1)} %cot_in.1), custom_call_target="tpu_custom_call" | custom-call | tf_op jit(solution)/shard_map/pallas_call | solution.py:346
  38.0 1.0 %shard_map.59 = (bf16[512,256]{1,0:T(8,128)(2,1)}, bf16[3,512,256]{2,1,0:T(8,128)(2,1)}, f32[32,256]{1,0:T(8,128)}) custom-call(bf16[512,256]{1,0:T(8,128)(2,1)S(1)} %get-tuple-element.9.mixed, bf16[3,512,256]{2,1,0:T(8,128)(2,1)S(1)} %get-tuple-element.10.pgrad, f32[32,256]{1,0:T(8,128)S(1)} %get-tuple-element.11.fgrad), custom_call_target="tpu_custom_call" | custom-call | tf_op jit(solution)/shard_map/pallas_call | solution.py:372

commit v6 on v5

--- a/solution.py
+++ b/solution.py
@@ -145,7 +145,8 @@
     pl.semaphore_wait(barrier, NC + ND - 2)
     for o in (6, 2, 5, 7, 1, 3, 4):
         fd_copy(o).start()
-    over(NC, lambda o: p_copy(o).start())
+    for o in (10, 6, 8, 9, 7, 11, 5, 12, 4, 13, 3, 14, 2, 15, 1):
+        p_copy(o).start()
     fd[dp] = fs[dp]
     for g, h, piece in pieces(product(me)):
         rp[g, me, h] = piece
@@ -167,10 +168,11 @@
     arrived(8)
     for s in range(8):
         ft[s] = fd[:, s, :]
-    for o in range(1, NC):
+    for o in (10, 6, 8, 9, 7, 11, 5, 12, 4, 13, 3, 14, 2, 15, 1):
         f_copy(o).start()
     for g in range(OWN):
-        over(NC, lambda o: q_copy(g, o).start())
+        for o in (10, 6, 8, 9, 7, 11, 5, 12, 4, 13, 3, 14, 2, 15, 1):
+            q_copy(g, o).start()
     fr[me] = ft[lax.div(me, 2)]
     arrived(6)
 
@@ -224,7 +226,8 @@
                 yb[g] = value
             else:
                 yb[g, d:] += value
-        over(NC, lambda o: y_copy(g, o).start())
+        for o in (10, 6, 8, 9, 7, 11, 5, 12, 4, 13, 3, 14, 2, 15, 1):
+            y_copy(g, o).start()
         cv[me, g] = yb[g, me]
 
     @pl.loop(0, OWN)
@@ -264,7 +267,8 @@
                 zb[g] = value
             else:
                 zb[g, : NC - d] += value
-        over(NC, lambda o: z_copy(g, o).start())
+        for o in (10, 6, 8, 9, 7, 11, 5, 12, 4, 13, 3, 14, 2, 15, 1):
+            z_copy(g, o).start()
         pv[me, g] = zb[g, me]
 
     arrived(1)
@@ -284,7 +288,7 @@
         total = total.reshape(NC, 2, HALF)
         for h in range(2):
             fo[:, 4 * h + j, :] = total[:, h, :]
-    for o in range(1, NC):
+    for o in (10, 6, 8, 9, 7, 11, 5, 12, 4, 13, 3, 14, 2, 15, 1):
         g_copy(o).start()
     fa[me] = fo[me]
 

time: 39.1 us -> 38.5 us (0.985)
  Pallas kernels: 38.4 us -> 37.8 us
    pallas_call x1, Pallas kernels: 37.4 us -> 36.8 us  [on_device(): pl.pallas_call(kernel, out_shape=(jax.ShapeDtypeStruct((rows, cols), BF16...]
where the time goes in v6:
time: 38.5 us; the launch traced here: 38.4 us
  Pallas kernels  37.8 us (98%)
  between operations  0.64 us (2%)
    pallas_call x1, Pallas kernels, on_device(): pl.pallas_call(kernel, out_shape=(jax.ShapeDtypeStruct((rows, cols), BF16...  36.8 us
    pallas_call x1, Pallas kernels, on_device(): pl.pallas_call(write_out, out_shape=[jax.ShapeDtypeStruct(x.shape, x.dtyp...  1 us

profile of v6, /device:TPU:1, one launch (start us, length us, event | category | flops | bytes accessed | tf_op | source)
XLA Modules:
  0.0 38.4 jit_solution(4764003270546630333)
XLA Ops:
  0.6 36.8 %shard_map.58 = (bf16[512,256]{1,0:T(8,128)(2,1)S(1)}, bf16[3,512,256]{2,1,0:T(8,128)(2,1)S(1)}, f32[32,256]{1,0:T(8,128)S(1)}) custom-call(bf16[3,512,256]{2,1,0:T(8,128)(2,1)} %proj_in.1, f32[32,256]{1,0:T(8,128)} %bitcast.2, bf16[512,256]{1,0:T(8,128)(2,1)} %cot_in.1), custom_call_target="tpu_custom_call" | custom-call | tf_op jit(solution)/shard_map/pallas_call | solution.py:350
  37.4 1.0 %shard_map.59 = (bf16[512,256]{1,0:T(8,128)(2,1)}, bf16[3,512,256]{2,1,0:T(8,128)(2,1)}, f32[32,256]{1,0:T(8,128)}) custom-call(bf16[512,256]{1,0:T(8,128)(2,1)S(1)} %get-tuple-element.9.mixed, bf16[3,512,256]{2,1,0:T(8,128)(2,1)S(1)} %get-tuple-element.10.pgrad, f32[32,256]{1,0:T(8,128)S(1)} %get-tuple-element.11.fgrad), custom_call_target="tpu_custom_call" | custom-call | tf_op jit(solution)/shard_map/pallas_call | solution.py:376

commit v7 on v6

--- a/solution.py
+++ b/solution.py
@@ -105,7 +105,7 @@
     barrier = pltpu.get_barrier_semaphore()
     for o in (6, 2, 5, 7, 1, 3, 4):
         pl.semaphore_signal(barrier, inc=1, device_id=(me, dp_peer(o)), device_id_type=MESH)
-    for o in range(1, NC):
+    for o in (10, 6, 8, 9, 7, 11, 5, 12, 4, 13, 3, 14, 2, 15, 1):
         pl.semaphore_signal(barrier, inc=1, device_id=(ctx_peer(o), dp), device_id_type=MESH)
     loads = [
         pltpu.make_async_copy(filt_in, filt, lsem.at[0]),

time: 38.5 us -> 38.6 us (level)
  no operation moved by 1% of the time
where the time goes in v7:
time: 38.6 us; the launch traced here: 38.4 us
  Pallas kernels  37.8 us (98%)
  between operations  0.64 us (2%)
    pallas_call x1, Pallas kernels, on_device(): pl.pallas_call(kernel, out_shape=(jax.ShapeDtypeStruct((rows, cols), BF16...  36.8 us
    pallas_call x1, Pallas kernels, on_device(): pl.pallas_call(write_out, out_shape=[jax.ShapeDtypeStruct(x.shape, x.dtyp...  1 us

profile of v7, /device:TPU:1, one launch (start us, length us, event | category | flops | bytes accessed | tf_op | source)
XLA Modules:
  0.0 38.4 jit_solution(7991162557276973846)
XLA Ops:
  0.6 36.8 %shard_map.58 = (bf16[512,256]{1,0:T(8,128)(2,1)S(1)}, bf16[3,512,256]{2,1,0:T(8,128)(2,1)S(1)}, f32[32,256]{1,0:T(8,128)S(1)}) custom-call(bf16[3,512,256]{2,1,0:T(8,128)(2,1)} %proj_in.1, f32[32,256]{1,0:T(8,128)} %bitcast.2, bf16[512,256]{1,0:T(8,128)(2,1)} %cot_in.1), custom_call_target="tpu_custom_call" | custom-call | tf_op jit(solution)/shard_map/pallas_call | solution.py:350
  37.4 1.0 %shard_map.59 = (bf16[512,256]{1,0:T(8,128)(2,1)}, bf16[3,512,256]{2,1,0:T(8,128)(2,1)}, f32[32,256]{1,0:T(8,128)}) custom-call(bf16[512,256]{1,0:T(8,128)(2,1)S(1)} %get-tuple-element.9.mixed, bf16[3,512,256]{2,1,0:T(8,128)(2,1)S(1)} %get-tuple-element.10.pgrad, f32[32,256]{1,0:T(8,128)S(1)} %get-tuple-element.11.fgrad), custom_call_target="tpu_custom_call" | custom-call | tf_op jit(solution)/shard_map/pallas_call | solution.py:376
